TPU v7x, 128 devices: a whole 4x4x4 slice. The times are simulated.
128 devices in a mesh: seq: 32 (over x, y, core), dp: 4 (over z).
Axes of the slice: x: 4, y: 4, z: 4, core: 2. Of those that a mesh axis runs over, the one named last changes fastest.
Arguments:
- queries: bfloat16 [4, 4096, 2048], P('dp', 'seq'), may hold values from -6 to 6
- keys_in: bfloat16 [4, 4096, 2048], P('dp', 'seq'), may hold values from -9 to 9
- values_in: bfloat16 [4, 4096, 2048], P('dp', 'seq'), may hold values from -6 to 6
- inputs: bfloat16 [4, 4096, 2048], P('dp', 'seq'), may hold values from -6 to 6
- target: bfloat16 [4, 4096, 2048], P('dp', 'seq'), may hold values from -4 to 4
- gate_weight: bfloat16 [2048, 16], replicated, may hold values from -0.125 to 0.125
- beta_bias: float32 [16], replicated, may hold values from -9 to 1.5
Outputs:
- output: bfloat16 [4, 4096, 2048], P('dp', 'seq')
- grad_queries: bfloat16 [4, 4096, 2048], P('dp', 'seq')
- grad_keys: bfloat16 [4, 4096, 2048], P('dp', 'seq')
- grad_values: bfloat16 [4, 4096, 2048], P('dp', 'seq')
- grad_weight: float32 [2048, 16], replicated
All inputs are finite; a program needn't handle non-finite values.
Results may differ from a plain program's by a relative error of at most 0.0035.
Values sent between devices are 32-bit elements; how exact they have to be, the bound alone decides.
A program may use at most 256 MiB of HBM per device.

v0:
```python
import math

import jax
import jax.numpy as jnp
from jax import lax
from jax.sharding import PartitionSpec as P

BLOCK = 128


epsilon = 1e-06
highest_precision = lax.Precision.HIGHEST


def carried_in(value, axis, join, neutral, backward):
    count, mine = (lax.axis_size(axis), lax.axis_index(axis))
    pieces = jax.tree.map(lambda part: lax.all_gather(part, axis), value)
    if backward:
        pieces = jax.tree.map(lambda part: part[::-1], pieces)
        mine = count - 1 - mine
    total = jax.tree.map(
        lambda part, zero: jnp.full_like(part, 0) + jnp.asarray(zero, part.dtype), value, neutral
    )

    def lap(position, total):
        longer = join(total, jax.tree.map(lambda part: part[position], pieces))
        return jax.tree.map(lambda new, old: jnp.where(position < mine, new, old), longer, total)

    return lax.fori_loop(0, count - 1, lap, total)


def unit_rows(matrix):
    return matrix * lax.rsqrt(jnp.sum(matrix * matrix, axis=-1, keepdims=True) + epsilon)


def block_terms(queries, keys_in, values_in, logits):
    length = queries.shape[0]
    head_count = logits.shape[1]
    head_width = queries.shape[1] // head_count
    blocks = length // BLOCK

    def arrange(matrix):
        return matrix.reshape(blocks, BLOCK, head_count, head_width).transpose(0, 2, 1, 3)

    query_unit = unit_rows(arrange(queries.astype(jnp.float32)))
    key_unit = unit_rows(arrange(keys_in.astype(jnp.float32)))
    value_rows = arrange(values_in.astype(jnp.float32))
    strength = (
        (0.5 * jax.nn.sigmoid(logits))
        .reshape(blocks, BLOCK, head_count)
        .transpose(0, 2, 1)[..., None]
    )
    key_gram = jnp.einsum("nhik,nhjk->nhij", key_unit, key_unit, precision=highest_precision)
    lower_mask = jnp.tril(jnp.ones((BLOCK, BLOCK), jnp.float32), -1)
    system = jnp.eye(BLOCK, dtype=jnp.float32) + lower_mask * strength * key_gram
    right_side = jnp.concatenate([strength * key_unit, strength * value_rows], axis=-1)
    solved = jax.scipy.linalg.solve_triangular(system, right_side, lower=True)
    write_keys = solved[..., :head_width]
    write_values = solved[..., head_width:]
    inclusive = jnp.tril(jnp.ones((BLOCK, BLOCK), jnp.float32))
    scores = inclusive * jnp.einsum(
        "nhik,nhjk->nhij", query_unit, key_unit, precision=highest_precision
    )
    return (query_unit, key_unit, write_keys, write_values, scores)


def state_pass(terms, entry_state):

    def state_advance(carried_state, block_parts):
        block_queries, block_keys, write_keys, write_values, score_block = block_parts
        delta_correction = write_values - jnp.einsum(
            "fbi,fir->fbr", write_keys, carried_state, precision=highest_precision
        )
        produced_output = jnp.einsum(
            "fbi,fir->fbr", block_queries, carried_state, precision=highest_precision
        )
        produced_output = produced_output + jnp.einsum(
            "hcj,hjv->hcv", score_block, delta_correction, precision=highest_precision
        )
        carried_state = carried_state + jnp.einsum(
            "nrm,nrp->nmp", block_keys, delta_correction, precision=highest_precision
        )
        return (carried_state, produced_output)

    final_state, produced_output = lax.scan(state_advance, entry_state, terms)
    blocks, head_count, rows_block, head_width = produced_output.shape
    flat = produced_output.transpose(0, 2, 1, 3).reshape(
        blocks * rows_block, head_count * head_width
    )
    return (flat, final_state)


def transition_maps(terms, identity):
    query_unit, key_unit, write_keys, write_values, scores = terms
    head_width = identity.shape[-1]
    joined = jnp.concatenate([identity, jnp.zeros_like(identity)], axis=-1)

    def transition_advance(carried_state, block_parts):
        block_keys, key_portion, value_part = block_parts
        written_update = jnp.concatenate([jnp.zeros_like(value_part), value_part], axis=-1)
        delta_correction = written_update - jnp.einsum(
            "fbi,fir->fbr", key_portion, carried_state, precision=highest_precision
        )
        carried_state = carried_state + jnp.einsum(
            "nrm,nrp->nmp", block_keys, delta_correction, precision=highest_precision
        )
        return (carried_state, None)

    joined = lax.scan(transition_advance, joined, (key_unit, write_keys, write_values))[0]
    return (joined[..., :head_width], joined[..., head_width:])


def apply_map(matrix, offset, carried_state):
    return jnp.einsum("hij,hjk->hik", matrix, carried_state, precision=highest_precision) + offset


def compose(earlier, later):
    matrix = jnp.einsum("hij,hjk->hik", later[0], earlier[0], precision=highest_precision)
    return (matrix, apply_map(later[0], later[1], earlier[1]))


def shards(queries, keys_in, values_in, inputs, target, gate_weight, beta_bias):
    query_rows = queries[0]
    key_rows = keys_in[0]
    value_rows = values_in[0]
    input_rows = inputs[0]
    target_rows = target[0]
    head_count = gate_weight.shape[1]
    head_width = query_rows.shape[1] // head_count
    logits = jnp.dot(input_rows, gate_weight, preferred_element_type=jnp.float32) + beta_bias
    terms, pull_terms = jax.vjp(block_terms, query_rows, key_rows, value_rows, logits)
    identity = jnp.broadcast_to(
        jnp.eye(head_width, dtype=jnp.float32), (head_count, head_width, head_width)
    )
    zero_state = jnp.zeros((head_count, head_width, head_width), jnp.float32)
    transition, offset = transition_maps(terms, identity)
    entry_state = carried_in((transition, offset), "seq", compose, (identity, zero_state), False)[1]
    (produced_output, final_state), pull_state = jax.vjp(state_pass, terms, entry_state)
    rounded = lax.optimization_barrier(produced_output.astype(jnp.bfloat16))
    cotangent = rounded.astype(jnp.float32) - target_rows.astype(jnp.float32)
    pull_entry = jax.vjp(lambda carried_state: state_pass(terms, carried_state)[0], entry_state)[1]
    entry_grad = pull_entry(cotangent)[0]
    adjoint = jnp.swapaxes(transition, 1, 2)
    leaving = carried_in((adjoint, entry_grad), "seq", compose, (identity, zero_state), True)[1]
    grad_terms = pull_state((cotangent, leaving))[0]
    grad_q, grad_k, grad_v, grad_logits = pull_terms(grad_terms)
    local_weight = jnp.dot(
        input_rows.T, grad_logits, preferred_element_type=jnp.float32, precision=highest_precision
    )
    weight_total = lax.psum(local_weight, ("seq", "dp"))
    token_count = input_rows.shape[0] * lax.axis_size("seq") * lax.axis_size("dp")
    scaled = weight_total * (1.0 / math.sqrt(token_count))
    return (rounded[None], grad_q[None], grad_k[None], grad_v[None], scaled)


def solution(mesh):
    placed = (
        P("dp", "seq", None),
        P("dp", "seq", None),
        P("dp", "seq", None),
        P("dp", "seq", None),
        P("dp", "seq", None),
        P(),
        P(),
    )
    return jax.shard_map(
        shards,
        mesh=mesh,
        in_specs=placed,
        out_specs=(
            P("dp", "seq", None),
            P("dp", "seq", None),
            P("dp", "seq", None),
            P("dp", "seq", None),
            P(),
        ),
        check_vma=False,
    )
```

profile of v0, /device:TPU:1, one launch (start us, length us, event | category | flops | bytes accessed | tf_op | source)
XLA Modules:
  0.0 998.0 jit_solution(9470299216437238862)
XLA Ops:
  14.5 158.8 %custom-call.10 = f32[16,1,128,128]{2,3,1,0:T(8,128)} custom-call(f32[16,1,128,128]{3,2,1,0:T(8,128)} %fusion.46), custom_call_target="InvertDiagBlocksLowerTriangular" | custom-call | tf_op jit(solution)/shard_map/jvp(jit(_solve_triangular))/vmap()/triangular_solve | solution.py:57
  187.2 4.5 convolution_multiply_fusion.1
  191.7 110.8 %all-gather.9.cloned.1.call-done = f32[512,128,128]{2,1,0:T(8,128)} async-done(((f32[16,128,128]{2,1,0:T(8,128)}), f32[512,128,128]{2,1,0:T(8,128)}) %all-gather.9.cloned.1.call-update) | async-done | bytes 33554448 | tf_op jit(solution)/shard_map/all_gather | solution.py:17
  302.5 115.3 %all-gather.11.cloned.1.call-done = f32[512,128,128]{2,1,0:T(8,128)} async-done(((f32[16,128,128]{2,1,0:T(8,128)}), f32[512,128,128]{2,1,0:T(8,128)}) %all-gather.11.cloned.1.call-update) | async-done | bytes 33554448 | tf_op jit(solution)/shard_map/all_gather | solution.py:17
  417.8 93.4 %while.18 = (s32[]{:T(128)}, f32[16,128,128]{2,1,0:T(8,128)S(1)}, s32[]{:T(128)}, f32[32,16,128,128]{3,2,1,0:T(8,128)}, f32[32,16,128,128]{3,2,1,0:T(8,128)}, /*index=5*/s32[]{:T(128)}, s32[]{:T(128)}) while((s32[]{:T(128)}, f32[16,128,128]{2,1,0:T(8,128)S(1)}, s32[]{:T(128)}, f32[32,16,128,128]{3,2,1,0:T(8,128)}, ...), condition=%wide.region_3.4_spmd.clone, body=%wide.region_2.3_spmd.clone.sunk | while | flops 403701760 | bytes 7342687 | solution.py:29
  533.1 23.3 %rev.6 = f32[32,16,128,128]{3,2,1,0:T(8,128)} reverse(f32[32,16,128,128]{3,2,1,0:T(8,128)} %bitcast.240), dimensions={0} | reverse | bytes 67108864 | tf_op jit(solution)/shard_map/rev | solution.py:19
  556.5 3.9 fusion.56
  566.3 82.0 %all-gather.15.cloned.1.call-done = f32[512,128,128]{2,1,0:T(8,128)} async-done(((f32[16,128,128]{2,1,0:T(8,128)}), f32[512,128,128]{2,1,0:T(8,128)}) %all-gather.15.cloned.1.call-update) | async-done | bytes 33554448 | tf_op jit(solution)/shard_map/all_gather | solution.py:17
  648.3 23.0 %rev.7 = f32[32,16,128,128]{3,2,1,0:T(8,128)} reverse(f32[32,16,128,128]{3,2,1,0:T(8,128)} %bitcast.241), dimensions={0} | reverse | bytes 67108864 | tf_op jit(solution)/shard_map/rev | solution.py:19
  671.3 155.4 %while.19 = (s32[]{:T(128)}, f32[16,128,128]{2,1,0:T(8,128)}, s32[]{:T(128)}, f32[32,16,128,128]{3,2,1,0:T(8,128)}, f32[32,16,128,128]{3,2,1,0:T(8,128)}, /*index=5*/s32[]{:T(128)}, s32[]{:T(128)}) while((s32[]{:T(128)}, f32[16,128,128]{2,1,0:T(8,128)}, s32[]{:T(128)}, f32[32,16,128,128]{3,2,1,0:T(8,128)}, ...), condition=%wide.region_6.7_spmd.clone, body=%wide.region_5.6_spmd.clone.sunk | while | flops 403701760 | bytes 7342687 | solution.py:29
  672.5 3.8 fusion.147
  677.5 3.8 fusion.147
  682.5 3.8 fusion.147
  692.6 3.8 fusion.147
  697.6 3.8 fusion.147
  717.6 3.8 fusion.147
  722.6 3.8 fusion.147
  747.7 3.8 fusion.147
  752.7 3.8 fusion.147
  777.7 3.8 fusion.147
  782.7 3.8 fusion.147
  807.8 3.8 fusion.147
  812.8 3.8 fusion.147
  854.0 135.7 %all-reduce.6.cloned.1.call-done = f32[2048,16]{0,1:T(8,128)} async-done(((f32[2048,16]{0,1:T(8,128)}), f32[2048,16]{0,1:T(8,128)}) %all-reduce.6.cloned.1.call-update) | async-done | bytes 131088 | tf_op jit(solution)/shard_map/psum | solution.py:150
  (241 shorter events, 275.3 us)
Async XLA Ops:
  7.2 5.0 copy-start
  7.2 2.1 copy-start.27
  7.2 295.3 %all-gather.9.cloned.1.call-start = ((), (), s32[]{:S(2)}) async-start(), calls=%async_computation.1 | async-start | bytes 34603008 | tf_op jit(solution)/shard_map/all_gather | solution.py:17
  9.3 2.9 copy-start.28
  9.3 2.9 copy-start.29
  9.5 5.0 copy-start.1
  185.0 232.8 %all-gather.11.cloned.1.call-start = ((), (), s32[]{:S(2)}) async-start(), calls=%async_computation.2 | async-start | bytes 34603008 | tf_op jit(solution)/shard_map/all_gather | solution.py:17
  185.7 347.4 %all-gather.13.cloned.1.call-start = ((), (), s32[]{:S(2)}) async-start(), calls=%async_computation.3 | async-start | bytes 34603008 | tf_op jit(solution)/shard_map/all_gather | solution.py:17
  187.1 461.2 %all-gather.15.cloned.1.call-start = ((), (), s32[]{:S(2)}) async-start(), calls=%async_computation.4 | async-start | bytes 34603008 | tf_op jit(solution)/shard_map/all_gather | solution.py:17
  511.2 2.9 copy-start.2
  514.1 3.8 copy-start.12
  520.8 2.2 copy-start.10
  520.8 2.2 copy-start.3
  523.0 2.6 copy-start.21
  529.7 460.0 %all-reduce.6.cloned.1.call-start = ((), (), s32[]{:S(2)}) async-start(), calls=%async_computation | async-start | bytes 262144 | tf_op jit(solution)/shard_map/psum | solution.py:150
  556.5 3.9 copy-start.11
  556.5 3.9 copy-start.13
  560.4 2.5 copy-start.4
  562.9 2.2 copy-start.15
  826.7 3.0 copy-start.6
  826.8 3.0 copy-start.14
  832.1 2.3 copy-start.20
  836.3 2.3 copy-start.23
  844.9 2.5 copy-start.25
  (11 other events, 16.8 us)
Sparse Core Ops, SparseCore 0:
  185.1 117.3 all-gather.8
  304.7 113.0 all-gather.10
  420.1 113.0 all-gather.12
  535.2 113.0 all-gather.14
  850.7 138.9 all-reduce.5
where the time goes:
time: 1000 us; the launch traced here: 998 us
  waiting for transfers between devices  448 us (45%)
  matrix products  264 us (26%)
  other arithmetic  168 us (17%)
  local copies, waits for them, and re-layouts  102 us (10%)
  between operations  14.7 us (1%)
    all_gather x4, waiting for transfers between devices, carried_in(): pieces = jax.tree.map(lambda part: lax.all_gather(part, axis), value)  311 us
    dot_general x62, matrix products, apply_map(): jnp.einsum('hij,hjk->hik', matrix, carried_state, precision=highest_preci...  207 us
    another operation x3, other arithmetic, block_terms(): solved = jax.scipy.linalg.solve_triangular(system, right_side, lower=True)  160 us
    psum x1, waiting for transfers between devices, shards(): weight_total = lax.psum(local_weight, ('seq', 'dp'))  136 us
    rev x2, local copies, waits for them, and re-layouts, carried_in(): pieces = jax.tree.map(lambda part: part[::-1], pieces)  46.3 us
    while x62, local copies, waits for them, and re-layouts  40.4 us
  transfers between devices with their start and end apart: 5, of which 5 were waited for; matrix products, arithmetic and copies ran while one was open for 15% of the time, Pallas kernels for 0%

commit v1 on v0

v1 whole, which is shorter than its diff:
```python
import functools
import math

import jax
import jax.numpy as jnp
from jax import lax
from jax.experimental import pallas as pl
from jax.experimental.pallas import tpu as pltpu
from jax.sharding import PartitionSpec as P

BLOCK = 128
EPSILON = 1e-06
GROUP = 4
f32 = jnp.float32
bf16 = jnp.bfloat16
MESH = pl.DeviceIdType.MESH


def mm(a, b):
    return jnp.dot(a, b, preferred_element_type=f32)


def mm_rows(a, b):
    return lax.dot_general(a, b, (((1,), (1,)), ((), ())), preferred_element_type=f32)


def mm3(a, b):
    return jnp.dot(a, b, preferred_element_type=f32, precision=lax.Precision.HIGH)


def split(x):
    high = x.astype(bf16)
    return high, (x - high.astype(f32)).astype(bf16)


def left_exact(exact, x):
    high, low = split(x)
    return mm(exact, high) + mm(exact, low)


def right_exact(x, exact):
    high, low = split(x)
    return mm(high, exact) + mm(low, exact)


def masks():
    row = lax.broadcasted_iota(jnp.int32, (BLOCK, BLOCK), 0)
    col = lax.broadcasted_iota(jnp.int32, (BLOCK, BLOCK), 1)
    return row, col


def unit_lower_inverse(systems):
    row, col = masks()
    apart = row ^ col
    eye = (row == col).astype(f32)
    inverses = [eye - jnp.where(apart < 2, a, 0.0) for a in systems]
    size = 2
    while size < BLOCK:
        band = (apart >= size) & (apart < 2 * size)
        packed = [x.astype(bf16) for x in inverses]
        steps = [mm(jnp.where(band, a, 0.0).astype(bf16), x) for a, x in zip(systems, packed)]
        steps = [mm(x, y.astype(bf16)) for x, y in zip(packed, steps)]
        inverses = [x - y for x, y in zip(inverses, steps)]
        size *= 2
    rest = [mm3(a, x) for a, x in zip(systems, inverses)]
    rest = [(eye - x - y) for x, y in zip(inverses, rest)]
    fixes = [mm(x.astype(bf16), y.astype(bf16)) for x, y in zip(inverses, rest)]
    return [x + y for x, y in zip(inverses, fixes)]


def kernel(
    chips,
    q_ref, k_ref, v_ref, x_ref, t_ref, w_ref, b_ref,
    o_ref, gq_ref, gk_ref, gv_ref, gw_ref,
    strength, rk_col, rq_col, be_col, rk_row,
    key_t, query_t, gram_s, inv_s, inv_t, wk_s, wv_s, p_s, p_t, z_s,
    f_s, f_t, s_t, do_s, e_s, dpq_s, dl_s,
    maps, out_map, chip_map, got_map, prefix, state_out, hand_in, state_in, s_own, s_sib, s_out,
    c_both, c_out, c_chip, c_got, suffix, map_t, grad_out, gh_in, grad_in, g_own, g_sib, g_out,
    send, recv,
):
    me = lax.axis_index("seq")
    core = lax.rem(me, 2)
    chip = lax.div(me, 2)
    half = chips // 2
    part = lax.div(chip, half)
    place = lax.rem(chip, half)
    parity = lax.rem(chip, 2)
    sibling = me + 1 - 2 * core
    rounds = half // min(GROUP, half)
    group = min(GROUP, half)

    def owner(j):
        return 2 * (2 * j + core) + part

    def source(i):
        return 2 * (half * core + i) + parity

    def push(kind, at, src, dst, target):
        return pltpu.make_async_remote_copy(
            src_ref=src, dst_ref=dst, send_sem=send.at[kind, at], recv_sem=recv.at[kind, at],
            device_id={"seq": target}, device_id_type=MESH,
        )

    def wait_in(kind, at, dst):
        push(kind, at, dst, dst, sibling).wait_recv()

    def route(kind, send_at, recv_at, src, dst, target):
        @pl.when(target != me)
        def _():
            pltpu.make_async_remote_copy(
                src_ref=src, dst_ref=dst, send_sem=send.at[kind, send_at], recv_sem=recv.at[kind, recv_at],
                device_id={"seq": target}, device_id_type=MESH,
            ).start()

        @pl.when(target == me)
        def _():
            dst[...] = src[...]

    def routed(kind, at, dst, origin):
        @pl.when(origin != me)
        def _():
            wait_in(kind, at, dst)

    barrier = pltpu.get_barrier_semaphore()

    def greet(target):
        @pl.when(target != me)
        def _():
            pl.semaphore_signal(barrier, inc=1, device_id={"seq": target}, device_id_type=MESH)

    pl.semaphore_signal(barrier, inc=1, device_id={"seq": sibling}, device_id_type=MESH)
    for j in range(half):
        greet(owner(j))
        greet(source(j))

    logits = mm(x_ref[...], w_ref[...]) + b_ref[...]
    strength[...] = 0.5 / (1.0 + jnp.exp(-logits))
    dl_s[...] = jnp.zeros_like(dl_s)

    own_self = (part == core) & (parity == core)

    @pl.when(own_self)
    def _():
        pl.semaphore_wait(barrier, 2 * half - 1)

    @pl.when(jnp.logical_not(own_self))
    def _():
        pl.semaphore_wait(barrier, 2 * half + 1)

    def span(head):
        return pl.ds(pl.multiple_of(head * BLOCK, BLOCK), BLOCK)

    def own_head(j):
        return 2 * j + core

    def other_head(j):
        return 2 * j + 1 - core

    def local_maps(slots, heads):
        row, col = masks()
        eye = row == col
        keys = [k_ref[:, span(h)] for h in heads]
        values = [v_ref[:, span(h)] for h in heads]
        strengths = strength[...]
        lane = lax.broadcasted_iota(jnp.int32, strengths.shape, 1)
        products = [mm_rows(key, key) for key in keys]
        norms = [jnp.where(eye, product, 0.0) for product in products]
        rks = [lax.rsqrt(jnp.sum(n, axis=1, keepdims=True) + EPSILON) for n in norms]
        rkr = [lax.rsqrt(jnp.sum(n, axis=0, keepdims=True) + EPSILON) for n in norms]
        bes = [jnp.sum(jnp.where(lane == h, strengths, 0.0), axis=1, keepdims=True) for h in heads]
        ber = [jnp.sum(jnp.where(eye, be, 0.0), axis=0, keepdims=True) for be in bes]
        grams = [jnp.where(row > col, m * a * b, 0.0) for m, a, b in zip(products, rks, rkr)]
        inverses = unit_lower_inverse([g * be for g, be in zip(grams, bes)])
        weights = [x * b for x, b in zip(inverses, ber)]
        wks = [right_exact(w * r, key) for w, r, key in zip(weights, rkr, keys)]
        wvs = [right_exact(w, value) for w, value in zip(weights, values)]
        keys_t = [key.T for key in keys]
        both = [
            left_exact(kt, jnp.concatenate([a, b], axis=1) * r) for kt, a, b, r in zip(keys_t, wks, wvs, rks)
        ]
        for i, s in enumerate(slots):
            rk_col[s] = rks[i]
            be_col[s] = bes[i]
            rk_row[s] = rkr[i]
            gram_s[s] = grams[i]
            inv_s[s] = inverses[i]
            wk_s[s] = wks[i]
            wv_s[s] = wvs[i]
            key_t[s] = keys_t[i]
        eyef = eye.astype(f32)
        return [jnp.concatenate([eyef - m[:, :BLOCK], m[:, BLOCK:]], axis=1) for m in both]

    def steps(body):
        def run(r, carry):
            body([r * group + u for u in range(group)])
            return carry

        lax.fori_loop(0, rounds, run, 0)

    def first_other(js):
        made = local_maps([half + j for j in js], [other_head(j) for j in js])
        for j, m in zip(js, made):
            out_map[j] = m
        for j in js:
            push(0, j, out_map.at[j], maps.at[core, j], sibling).start()

    steps(first_other)

    def first_own(js):
        made = local_maps(js, [own_head(j) for j in js])
        for j, m in zip(js, made):
            maps[core, j] = m
        for j in js:
            wait_in(0, j, maps.at[1 - core, j])
        zero = jnp.zeros((BLOCK, BLOCK), f32)
        earlier = [maps[0, j] for j in js]
        later = [maps[1, j] for j in js]
        made = [mm3(b[:, :BLOCK], a) for a, b in zip(earlier, later)]
        for j, m, b in zip(js, made, later):
            chip_map[j] = m + jnp.concatenate([zero, b[:, BLOCK:]], axis=1)
        for j in js:
            route(1, j, place, chip_map.at[j], got_map.at[place], owner(j))

    steps(first_own)

    def score_terms(slots, heads):
        row, col = masks()
        keys = [k_ref[:, span(h)] for h in heads]
        queries = [q_ref[:, span(h)] for h in heads]
        rkr = [rk_row[s] for s in slots]
        products = [mm_rows(q, k) for q, k in zip(queries, keys)]
        wide = [q.astype(f32) for q in queries]
        rqs = [lax.rsqrt(jnp.sum(q * q, axis=1, keepdims=True) + EPSILON) for q in wide]
        ps = [jnp.where(row >= col, m * a * b, 0.0) for m, a, b in zip(products, rqs, rkr)]
        inverses_t = [inv_s[s].T for s in slots]
        zs = [right_exact(x * r, k) for x, r, k in zip(inverses_t, rkr, keys)]
        for i, s in enumerate(slots):
            rq_col[s] = rqs[i]
            p_s[s] = ps[i]
            p_t[s] = ps[i].T
            inv_t[s] = inverses_t[i]
            z_s[s] = zs[i]
            query_t[s] = queries[i].T

    steps(lambda js: score_terms(js, [own_head(j) for j in js]))
    steps(lambda js: score_terms([half + j for j in js], [other_head(j) for j in js]))

    row, col = masks()
    eyef = (row == col).astype(f32)
    zero = jnp.zeros((BLOCK, BLOCK), f32)

    slot = lax.div(chip, 2)

    @pl.when(core == 0)
    def _():
        state_out[0] = zero

        def lap(i, carry):
            routed(1, i, got_map.at[i], source(i))
            route(3, i, slot, state_out.at[i], state_in.at[slot], source(i))
            step = got_map[i]
            state_out[i + 1] = mm3(step[:, :BLOCK], state_out[i]) + step[:, BLOCK:]
            return carry

        lax.fori_loop(0, half, lap, 0)
        push(2, 0, state_out.at[half], hand_in.at[0], sibling).start()
        suffix[half] = eyef

        def back(n, carry):
            i = half - 1 - n
            turned = got_map[i][:, :BLOCK].T
            map_t[i] = turned
            suffix[i] = mm3(turned, suffix[i + 1])
            return carry

        lax.fori_loop(0, half, back, 0)

    @pl.when(core == 1)
    def _():
        prefix[0] = jnp.concatenate([eyef, zero], axis=1)

        def lap(i, carry):
            routed(1, i, got_map.at[i], source(i))
            step = got_map[i]
            map_t[i] = step[:, :BLOCK].T
            prefix[i + 1] = mm3(step[:, :BLOCK], prefix[i]) + jnp.concatenate([zero, step[:, BLOCK:]], axis=1)
            return carry

        lax.fori_loop(0, half, lap, 0)
        wait_in(2, 0, hand_in.at[0])
        entry = hand_in[0]

        def lift(r, carry):
            for u in range(group):
                i = r * group + u
                known = prefix[i]
                state_out[i] = mm3(known[:, :BLOCK], entry) + known[:, BLOCK:]
            for u in range(group):
                i = r * group + u
                route(3, i, slot, state_out.at[i], state_in.at[slot], source(i))
            return carry

        lax.fori_loop(0, rounds, lift, 0)

    def enter(j, carry):
        routed(3, j, state_in.at[j], owner(j))
        first = state_in[j]
        step = maps[0, j]
        second = mm3(step[:, :BLOCK], first) + step[:, BLOCK:]
        s_own[j] = jnp.where(core == 0, first, second)
        s_out[j] = jnp.where(core == 0, second, first)
        push(4, j, s_out.at[j], s_sib.at[j], sibling).start()
        return carry

    lax.fori_loop(0, half, enter, 0)

    def forward(slots, heads, states):
        queries = [q_ref[:, span(h)] for h in heads]
        rqs = [rq_col[s] for s in slots]
        fresh = [wv_s[s] - mm3(wk_s[s], state) for s, state in zip(slots, states)]
        read = [left_exact(q, state) * r for q, state, r in zip(queries, states, rqs)]
        outs = [o + mm3(p_s[s], f) for o, f, s in zip(read, fresh, slots)]
        outs = [o.astype(bf16) for o in outs]
        cots = [o.astype(f32) - t_ref[:, span(h)].astype(f32) for o, h in zip(outs, heads)]
        ups = [mm3(p_t[s], d) for d, s in zip(cots, slots)]
        es = [mm3(inv_t[s], u) for u, s in zip(ups, slots)]
        cs = [left_exact(query_t[s], d * r) for s, d, r in zip(slots, cots, rqs)]
        cs = [c - left_exact(key_t[s], e * (rk_col[s] * be_col[s])) for c, s, e in zip(cs, slots, es)]
        for i, (s, h) in enumerate(zip(slots, heads)):
            o_ref[:, span(h)] = outs[i]
            f_s[s] = fresh[i]
            do_s[s] = cots[i]
            e_s[s] = es[i]
        return cs

    def second_own(js):
        made = forward(js, [own_head(j) for j in js], [s_own[j] for j in js])
        for j, c in zip(js, made):
            c_both[core, j] = c

    steps(second_own)

    def second_other(js):
        for j in js:
            wait_in(4, j, s_sib.at[j])
        made = forward([half + j for j in js], [other_head(j) for j in js], [s_sib[j] for j in js])
        for j, c in zip(js, made):
            c_out[j] = c
        for j in js:
            push(5, j, c_out.at[j], c_both.at[core, j], sibling).start()

    steps(second_other)

    def join_grads(js):
        for j in js:
            wait_in(5, j, c_both.at[1 - core, j])
        made = [mm3(maps[0, j][:, :BLOCK].T, c_both[1, j]) + c_both[0, j] for j in js]
        for j, c in zip(js, made):
            c_chip[j] = c
        for j in js:
            route(6, j, place, c_chip.at[j], c_got.at[place], owner(j))

    steps(join_grads)

    def query_grads(slots, heads, states):
        row, col = masks()
        fts = [f_s[s].T for s in slots]
        sts = [state.T for state in states]
        cots = [do_s[s] for s in slots]
        rqs = [rq_col[s] for s in slots]
        dps = [jnp.where(row >= col, mm3(d, ft), 0.0) for d, ft in zip(cots, fts)]
        dqs = [mm3(d, st) for d, st in zip(cots, sts)]
        dqs = [
            d + right_exact(p * rk_row[s], k_ref[:, span(h)]) for d, p, s, h in zip(dqs, dps, slots, heads)
        ]
        turned = [right_exact((p * r).T, q_ref[:, span(h)]) for p, r, h in zip(dps, rqs, heads)]
        for i, (s, h) in enumerate(zip(slots, heads)):
            unit = q_ref[:, span(h)].astype(f32) * rqs[i]
            grad = rqs[i] * (dqs[i] - unit * jnp.sum(unit * dqs[i], axis=1, keepdims=True))
            gq_ref[:, span(h)] = grad.astype(bf16)
            dpq_s[s] = turned[i]
            f_t[s] = fts[i]
            s_t[s] = sts[i]

    steps(lambda js: query_grads(js, [own_head(j) for j in js], [s_own[j] for j in js]))
    steps(
        lambda js: query_grads(
            [half + j for j in js], [other_head(j) for j in js], [s_sib[j] for j in js]
        )
    )

    grad_out[half] = zero

    @pl.when(core == 1)
    def _():
        def lap(n, carry):
            i = half - 1 - n
            routed(6, i, c_got.at[i], source(i))
            route(8, i, slot, grad_out.at[i + 1], grad_in.at[slot], source(i))
            grad_out[i] = mm3(map_t[i], grad_out[i + 1]) + c_got[i]
            return carry

        lax.fori_loop(0, half, lap, 0)
        push(7, 0, grad_out.at[0], gh_in.at[0], sibling).start()

    @pl.when(core == 0)
    def _():
        def lap(n, carry):
            i = half - 1 - n
            routed(6, i, c_got.at[i], source(i))
            grad_out[i] = mm3(map_t[i], grad_out[i + 1]) + c_got[i]
            return carry

        lax.fori_loop(0, half, lap, 0)
        wait_in(7, 0, gh_in.at[0])
        entry = gh_in[0]

        def lift(r, carry):
            for u in range(group):
                i = half - 1 - (r * group + u)
                grad_out[i + 1] = mm3(suffix[i + 1], entry) + grad_out[i + 1]
            for u in range(group):
                i = half - 1 - (r * group + u)
                route(8, i, slot, grad_out.at[i + 1], grad_in.at[slot], source(i))
            return carry

        lax.fori_loop(0, rounds, lift, 0)

    def leave(j, carry):
        routed(8, j, grad_in.at[j], owner(j))
        last = grad_in[j]
        inner = mm3(maps[1, j][:, :BLOCK].T, last) + c_both[1, j]
        g_own[j] = jnp.where(core == 0, inner, last)
        g_out[j] = jnp.where(core == 0, last, inner)
        push(9, j, g_out.at[j], g_sib.at[j], sibling).start()
        return carry

    lax.fori_loop(0, half, leave, 0)

    def backward(slots, heads, grads):
        row, col = masks()
        es = [e_s[s] + mm3(z_s[s], g) for s, g in zip(slots, grads)]
        gts = [g.T for g in grads]
        efs = [jnp.where(row > col, mm3(e, f_t[s]), 0.0) for e, s in zip(es, slots)]
        ess = [mm3(e, s_t[s]) for e, s in zip(es, slots)]
        dks = [dpq_s[s] + mm3(f_s[s], gt) for s, gt in zip(slots, gts)]
        bes = [be_col[s] for s in slots]
        links = [ef * be for ef, be in zip(efs, bes)]
        links = [(m + m.T) * rk_row[s] for m, s in zip(links, slots)]
        dks = [d - es_ * be for d, es_, be in zip(dks, ess, bes)]
        dks = [d - right_exact(m, k_ref[:, span(h)]) for d, m, h in zip(dks, links, heads)]
        added = 0.0
        lane = lax.broadcasted_iota(jnp.int32, (BLOCK, BLOCK), 1)
        for i, (s, h) in enumerate(zip(slots, heads)):
            rk = rk_col[s]
            unit = k_ref[:, span(h)].astype(f32) * rk
            grad = rk * (dks[i] - unit * jnp.sum(unit * dks[i], axis=1, keepdims=True))
            gk_ref[:, span(h)] = grad.astype(bf16)
            gv_ref[:, span(h)] = (es[i] * bes[i]).astype(bf16)
            terms = es[i] * v_ref[:, span(h)].astype(f32) - ess[i] * unit - efs[i] * gram_s[s]
            dl = jnp.sum(terms, axis=1, keepdims=True) * (bes[i] * (1.0 - 2.0 * bes[i]))
            added = added + jnp.where(lane == h, dl, 0.0)
        dl_s[...] += added

    steps(lambda js: backward(js, [own_head(j) for j in js], [g_own[j] for j in js]))

    def last_other(js):
        for j in js:
            wait_in(9, j, g_sib.at[j])
        backward([half + j for j in js], [other_head(j) for j in js], [g_sib[j] for j in js])

    steps(last_other)

    heads = 2 * half
    gate = dl_s[...].T
    high, low = split(gate[:heads])
    gw_ref[...] = mm(high, x_ref[...]) + mm(low, x_ref[...])

    def drain(j, carry):
        push(0, j, out_map.at[j], out_map.at[j], sibling).wait_send()
        push(4, j, s_out.at[j], s_out.at[j], sibling).wait_send()
        push(5, j, c_out.at[j], c_out.at[j], sibling).wait_send()
        push(9, j, g_out.at[j], g_out.at[j], sibling).wait_send()

        @pl.when(owner(j) != me)
        def _():
            push(1, j, chip_map.at[j], chip_map.at[j], sibling).wait_send()
            push(6, j, c_chip.at[j], c_chip.at[j], sibling).wait_send()

        @pl.when(source(j) != me)
        def _():
            push(3, j, state_out.at[j], state_out.at[j], sibling).wait_send()
            push(8, j, grad_out.at[j + 1], grad_out.at[j + 1], sibling).wait_send()

        return carry

    lax.fori_loop(0, half, drain, 0)

    @pl.when(core == 0)
    def _():
        push(2, 0, state_out.at[half], state_out.at[half], sibling).wait_send()

    @pl.when(core == 1)
    def _():
        push(7, 0, grad_out.at[0], grad_out.at[0], sibling).wait_send()


def shards(chips, queries, keys_in, values_in, inputs, target, gate_weight, beta_bias):
    heads = gate_weight.shape[1]
    width = heads * BLOCK
    half = heads // 2
    square = (BLOCK, BLOCK)

    def many(count, *tail, kind=f32):
        return pltpu.VMEM((count,) + (tail or square), kind)

    wide = (BLOCK, 2 * BLOCK)
    scratch = [
        pltpu.VMEM((BLOCK, heads), f32), many(heads, BLOCK, 1), many(heads, BLOCK, 1), many(heads, BLOCK, 1),
        many(heads, 1, BLOCK),
        many(heads, kind=bf16), many(heads, kind=bf16),
    ] + [many(heads)] * 8 + [many(heads)] * 6 + [
        pltpu.VMEM(square, f32),
        pltpu.VMEM((2, half) + wide, f32), many(half, *wide), many(half, *wide), many(half, *wide),
        many(half + 1, *wide), many(half + 1), many(1), many(half), many(half), many(half), many(half),
        pltpu.VMEM((2, half) + square, f32), many(half), many(half), many(half), many(half + 1), many(half),
        many(half + 1), many(1), many(half), many(half), many(half), many(half),
        pltpu.SemaphoreType.DMA((10, half)), pltpu.SemaphoreType.DMA((10, half)),
    ]
    rows = jax.ShapeDtypeStruct((BLOCK, width), bf16)
    whole = pl.BlockSpec(memory_space=pltpu.VMEM)
    results = pl.pallas_call(
        functools.partial(kernel, chips),
        out_shape=(rows, rows, rows, rows, jax.ShapeDtypeStruct((heads, inputs.shape[-1]), f32)),
        in_specs=[whole] * 7,
        out_specs=(whole,) * 5,
        scratch_shapes=scratch,
        compiler_params=pltpu.CompilerParams(
            collective_id=0, has_side_effects=True, vmem_limit_bytes=52 * 1024 * 1024
        ),
    )(queries[0], keys_in[0], values_in[0], inputs[0], target[0], gate_weight, beta_bias[None])
    output, grad_q, grad_k, grad_v, local_weight = results
    total = lax.psum(local_weight, ("seq", "dp"))
    tokens = BLOCK * lax.axis_size("seq") * lax.axis_size("dp")
    scaled = total.T * (1.0 / math.sqrt(tokens))
    return (output[None], grad_q[None], grad_k[None], grad_v[None], scaled)


def solution(mesh):
    placed = P("dp", "seq", None)
    chips = mesh.shape["seq"] // 2
    return jax.shard_map(
        functools.partial(shards, chips),
        mesh=mesh,
        in_specs=(placed,) * 5 + (P(), P()),
        out_specs=(placed,) * 4 + (P(),),
        check_vma=False,
    )
```

time: 1000 us -> 242 us (0.24)
  waiting for transfers between devices: 448 us -> 140 us
  matrix products: 264 us -> 0 us
  other arithmetic: 168 us -> 1.57 us
  local copies, waits for them, and re-layouts: 102 us -> 6.11 us
  Pallas kernels: 0 us -> 80.3 us
    all_gather x4 -> x0, waiting for transfers between devices: 311 us -> none  [carried_in(): pieces = jax.tree.map(lambda part: lax.all_gather(part, axis), value)]
    dot_general x85 -> x0, matrix products: 258 us -> none  [the longest x62 207 us: apply_map(): jnp.einsum('hij,hjk->hik', matrix, carried_state, precision=highest_preci...]
    another operation x3 -> x0, other arithmetic: 160 us -> none  [block_terms(): solved = jax.scipy.linalg.solve_triangular(system, right_side, lower=True)]
    pallas_call x0 -> x1, Pallas kernels: none -> 80.3 us  [shards(): pl.pallas_call(functools.partial(kernel, chips), out_shape=(rows, rows, r...]
    rev x2 -> x0, local copies, waits for them, and re-layouts: 46.3 us -> none  [carried_in(): pieces = jax.tree.map(lambda part: part[::-1], pieces)]
    while x62 -> x0, local copies, waits for them, and re-layouts: 40.4 us -> none
  transfers between devices with their start and end apart: 5 -> 1, of which waited for: 5 -> 1; matrix products, arithmetic and copies ran while one was open for 15% -> 0% of each run, Pallas kernels for 0% -> 0%
where the time goes in v1:
time: 242 us
  waiting for transfers between devices  140 us (58%)
  Pallas kernels  80.3 us (33%)
  between operations  14 us (6%)
  local copies, waits for them, and re-layouts  6.11 us (3%)
    psum x1, waiting for transfers between devices, shards(): total = lax.psum(local_weight, ('seq', 'dp'))  140 us
    pallas_call x1, Pallas kernels, shards(): pl.pallas_call(functools.partial(kernel, chips), out_shape=(rows, rows, r...  80.3 us
    unnamed x9, local copies, waits for them, and re-layouts  6.11 us
  transfers between devices with their start and end apart: 1, of which 1 were waited for; matrix products, arithmetic and copies ran while one was open for 0% of the time, Pallas kernels for 0%

profile of v1, /device:TPU:1, one launch (start us, length us, event | category | flops | bytes accessed | tf_op | source)
XLA Modules:
  0.0 241.8 jit_solution(2080631913043944442)
XLA Ops:
  7.2 0.0 all-reduce.2.cloned.1.call-start
  7.2 1.8 copy.12.w_ref
  9.1 0.0 copy-start
  9.1 0.7 copy-done
  9.7 80.3 %shard_map.110 = (bf16[128,2048]{1,0:T(8,128)(2,1)S(1)}, bf16[128,2048]{1,0:T(8,128)(2,1)S(1)}, bf16[128,2048]{1,0:T(8,128)(2,1)S(1)}, bf16[128,2048]{1,0:T(8,128)(2,1)}, f32[16,2048]{1,0:T(8,128)}) custom-call(bf16[128,2048]{1,0:T(8,128)(2,1)} %bitcast.17, bf16[128,2048]{1,0:T(8,128)(2,1)} %bitcast.18, bf16[128,2048]{1,0:T(8,128)(2,1)} %bitcast.19, ...), custom_call_target="tpu_custom_call" | custom-call | tf_op jit(solution)/shard_map/pallas_call | solution.py:533
  90.0 0.0 all-reduce.2.cloned.1.call-update
  90.0 139.7 %all-reduce.2.cloned.1.call-done = f32[16,2048]{1,0:T(8,128)} async-done(((f32[16,2048]{1,0:T(8,128)}), f32[16,2048]{1,0:T(8,128)}) %all-reduce.2.cloned.1.call-update) | async-done | bytes 131088 | tf_op jit(solution)/shard_map/psum | solution.py:544
  229.7 1.6 multiply_bitcast_fusion
  231.3 0.8 copy.18
  232.1 0.8 copy.19
  232.9 0.0 copy-start.1
  232.9 0.8 copy.20
  233.7 0.4 copy-done.1
  234.1 0.8 copy.21
Async XLA Ops:
  7.2 222.6 %all-reduce.2.cloned.1.call-start = ((), (), s32[]{:S(2)}) async-start(), calls=%async_computation | async-start | bytes 262144 | tf_op jit(solution)/shard_map/psum | solution.py:544
  9.1 0.7 copy-start
  232.9 1.2 copy-start.1
Sparse Core Ops, SparseCore 0:
  90.2 139.5 all-reduce.1

commit v2 on v1

--- a/solution.py
+++ b/solution.py
@@ -69,7 +69,7 @@
 
 
 def kernel(
-    chips,
+    chips, depth, scale,
     q_ref, k_ref, v_ref, x_ref, t_ref, w_ref, b_ref,
     o_ref, gq_ref, gk_ref, gv_ref, gw_ref,
     strength, rk_col, rq_col, be_col, rk_row,
@@ -77,7 +77,8 @@
     f_s, f_t, s_t, do_s, e_s, dpq_s, dl_s,
     maps, out_map, chip_map, got_map, prefix, state_out, hand_in, state_in, s_own, s_sib, s_out,
     c_both, c_out, c_chip, c_got, suffix, map_t, grad_out, gh_in, grad_in, g_own, g_sib, g_out,
-    send, recv,
+    gate_own, gate_other, gate_in, depth_out, depth_in, tile_out, tiles,
+    send, recv, gate_send, gate_recv, depth_send, depth_recv,
 ):
     me = lax.axis_index("seq")
     core = lax.rem(me, 2)
@@ -122,31 +123,24 @@
         def _():
             wait_in(kind, at, dst)
 
+    devices = 2 * chips
+    layer = lax.axis_index("dp")
+
+    def others(count, base, body, first=1):
+        def run(d, carry):
+            body(lax.rem(base + d, count))
+            return carry
+
+        lax.fori_loop(first, count, run, 0)
+
     barrier = pltpu.get_barrier_semaphore()
-
-    def greet(target):
-        @pl.when(target != me)
-        def _():
-            pl.semaphore_signal(barrier, inc=1, device_id={"seq": target}, device_id_type=MESH)
-
-    pl.semaphore_signal(barrier, inc=1, device_id={"seq": sibling}, device_id_type=MESH)
-    for j in range(half):
-        greet(owner(j))
-        greet(source(j))
-
-    logits = mm(x_ref[...], w_ref[...]) + b_ref[...]
+    others(devices, me, lambda t: pl.semaphore_signal(barrier, inc=1, device_id={"seq": t}, device_id_type=MESH))
+    others(depth, layer, lambda t: pl.semaphore_signal(barrier, inc=1, device_id={"dp": t}, device_id_type=MESH))
+
+    logits = mm_rows(x_ref[...], w_ref[...]) + b_ref[...]
     strength[...] = 0.5 / (1.0 + jnp.exp(-logits))
     dl_s[...] = jnp.zeros_like(dl_s)
-
-    own_self = (part == core) & (parity == core)
-
-    @pl.when(own_self)
-    def _():
-        pl.semaphore_wait(barrier, 2 * half - 1)
-
-    @pl.when(jnp.logical_not(own_self))
-    def _():
-        pl.semaphore_wait(barrier, 2 * half + 1)
+    pl.semaphore_wait(barrier, devices + depth - 2)
 
     def span(head):
         return pl.ds(pl.multiple_of(head * BLOCK, BLOCK), BLOCK)
@@ -460,10 +454,34 @@
             gv_ref[:, span(h)] = (es[i] * bes[i]).astype(bf16)
             terms = es[i] * v_ref[:, span(h)].astype(f32) - ess[i] * unit - efs[i] * gram_s[s]
             dl = jnp.sum(terms, axis=1, keepdims=True) * (bes[i] * (1.0 - 2.0 * bes[i]))
-            added = added + jnp.where(lane == h, dl, 0.0)
+            added = added + jnp.where(lane == s, dl, 0.0)
         dl_s[...] += added
 
     steps(lambda js: backward(js, [own_head(j) for j in js], [g_own[j] for j in js]))
+
+    def gate_copy(kind, at, src, target):
+        return pltpu.make_async_remote_copy(
+            src_ref=src, dst_ref=(tiles if kind == 2 else gate_in).at[me], send_sem=gate_send.at[kind, at],
+            recv_sem=gate_recv.at[kind // 2, me], device_id={"seq": target}, device_id_type=MESH,
+        )
+
+    def gate_wait(kind, dst, origin):
+        pltpu.make_async_remote_copy(
+            src_ref=dst, dst_ref=dst, send_sem=gate_send.at[kind, 0],
+            recv_sem=gate_recv.at[kind, origin], device_id={"seq": sibling}, device_id_type=MESH,
+        ).wait_recv()
+
+    def gate_rows(first, tiles_ref):
+        rows = dl_s[...].T[first : first + half]
+        parts = jnp.concatenate([rows, rows - rows.astype(bf16).astype(f32)], axis=0).astype(bf16)
+        product = mm(parts, x_ref[...])
+        product = product[:half] + product[half:]
+        for c in range(chips):
+            tiles_ref[c] = product[:, c * BLOCK : (c + 1) * BLOCK]
+
+    gate_rows(0, gate_own)
+    gate_in[me] = gate_own[chip]
+    others(chips, chip, lambda c: gate_copy(0, c, gate_own.at[c], 2 * c + core).start())
 
     def last_other(js):
         for j in js:
@@ -472,10 +490,47 @@
 
     steps(last_other)
 
-    heads = 2 * half
-    gate = dl_s[...].T
-    high, low = split(gate[:heads])
-    gw_ref[...] = mm(high, x_ref[...]) + mm(low, x_ref[...])
+    gate_rows(half, gate_other)
+    others(chips, chip, lambda c: gate_copy(1, c, gate_other.at[c], 2 * c + 1 - core).start(), first=0)
+    others(devices, me, lambda t: gate_wait(0, gate_in.at[t], t))
+    total = gate_in[0]
+    for t in range(1, devices):
+        total = total + gate_in[t]
+    depth_out[0] = total
+    depth_in[layer] = total
+
+    def depth_copy(t, dst):
+        return pltpu.make_async_remote_copy(
+            src_ref=depth_out.at[0], dst_ref=dst, send_sem=depth_send.at[t],
+            recv_sem=depth_recv.at[layer], device_id={"dp": t}, device_id_type=MESH,
+        )
+
+    def depth_wait(t):
+        pltpu.make_async_remote_copy(
+            src_ref=depth_out.at[0], dst_ref=depth_in.at[t], send_sem=depth_send.at[t],
+            recv_sem=depth_recv.at[t], device_id={"dp": t}, device_id_type=MESH,
+        ).wait_recv()
+
+    others(depth, layer, lambda t: depth_copy(t, depth_in.at[layer]).start())
+    others(depth, layer, depth_wait)
+    total = depth_in[0]
+    for t in range(1, depth):
+        total = total + depth_in[t]
+    total = total * scale
+    tile_out[0] = total
+    tiles[me] = total
+    others(devices, me, lambda t: gate_copy(2, t, tile_out.at[0], t).start())
+    others(devices, me, lambda t: gate_wait(1, tiles.at[t], t))
+    for t in range(devices):
+        tile = tiles[t]
+        for r in range(half):
+            at = 2 * r + t % 2
+            gw_ref[at : at + 1, (t // 2) * BLOCK : (t // 2 + 1) * BLOCK] = tile[r : r + 1]
+
+    others(chips, chip, lambda c: gate_copy(0, c, gate_own.at[c], sibling).wait_send())
+    others(chips, chip, lambda c: gate_copy(1, c, gate_other.at[c], sibling).wait_send(), first=0)
+    others(depth, layer, lambda t: depth_copy(t, depth_in.at[layer]).wait_send())
+    others(devices, me, lambda t: gate_copy(2, t, tile_out.at[0], sibling).wait_send())
 
     def drain(j, carry):
         push(0, j, out_map.at[j], out_map.at[j], sibling).wait_send()
@@ -506,7 +561,7 @@
         push(7, 0, grad_out.at[0], grad_out.at[0], sibling).wait_send()
 
 
-def shards(chips, queries, keys_in, values_in, inputs, target, gate_weight, beta_bias):
+def shards(chips, depth, queries, keys_in, values_in, inputs, target, gate_weight, beta_bias):
     heads = gate_weight.shape[1]
     width = heads * BLOCK
     half = heads // 2
@@ -526,12 +581,16 @@
         many(half + 1, *wide), many(half + 1), many(1), many(half), many(half), many(half), many(half),
         pltpu.VMEM((2, half) + square, f32), many(half), many(half), many(half), many(half + 1), many(half),
         many(half + 1), many(1), many(half), many(half), many(half), many(half),
+        many(chips, half, BLOCK), many(chips, half, BLOCK), many(2 * chips, half, BLOCK), many(1, half, BLOCK),
+        many(depth, half, BLOCK), many(1, half, BLOCK), many(2 * chips, half, BLOCK),
         pltpu.SemaphoreType.DMA((10, half)), pltpu.SemaphoreType.DMA((10, half)),
+        pltpu.SemaphoreType.DMA((3, 2 * chips)), pltpu.SemaphoreType.DMA((2, 2 * chips)),
+        pltpu.SemaphoreType.DMA((depth,)), pltpu.SemaphoreType.DMA((depth,)),
     ]
     rows = jax.ShapeDtypeStruct((BLOCK, width), bf16)
     whole = pl.BlockSpec(memory_space=pltpu.VMEM)
     results = pl.pallas_call(
-        functools.partial(kernel, chips),
+        functools.partial(kernel, chips, depth, 1.0 / math.sqrt(BLOCK * 2 * chips * depth)),
         out_shape=(rows, rows, rows, rows, jax.ShapeDtypeStruct((heads, inputs.shape[-1]), f32)),
         in_specs=[whole] * 7,
         out_specs=(whole,) * 5,
@@ -539,19 +598,16 @@
         compiler_params=pltpu.CompilerParams(
             collective_id=0, has_side_effects=True, vmem_limit_bytes=52 * 1024 * 1024
         ),
-    )(queries[0], keys_in[0], values_in[0], inputs[0], target[0], gate_weight, beta_bias[None])
-    output, grad_q, grad_k, grad_v, local_weight = results
-    total = lax.psum(local_weight, ("seq", "dp"))
-    tokens = BLOCK * lax.axis_size("seq") * lax.axis_size("dp")
-    scaled = total.T * (1.0 / math.sqrt(tokens))
-    return (output[None], grad_q[None], grad_k[None], grad_v[None], scaled)
+    )(queries[0], keys_in[0], values_in[0], inputs[0], target[0], gate_weight.T, beta_bias[None])
+    output, grad_q, grad_k, grad_v, grad_w = results
+    return (output[None], grad_q[None], grad_k[None], grad_v[None], grad_w.T)
 
 
 def solution(mesh):
     placed = P("dp", "seq", None)
     chips = mesh.shape["seq"] // 2
     return jax.shard_map(
-        functools.partial(shards, chips),
+        functools.partial(shards, chips, mesh.shape["dp"]),
         mesh=mesh,
         in_specs=(placed,) * 5 + (P(), P()),
         out_specs=(placed,) * 4 + (P(),),

time: 242 us -> 104 us (0.43)
  waiting for transfers between devices: 140 us -> 0 us
  Pallas kernels: 80.3 us -> 97.8 us
  between operations: 14 us -> 0.65 us
    psum x1 -> x0, waiting for transfers between devices: 140 us -> none  [shards(): total = lax.psum(local_weight, ('seq', 'dp'))]
    pallas_call x1, Pallas kernels: 80.3 us -> 97.8 us  [shards(): pl.pallas_call(functools.partial(kernel, chips, depth, 1.0 / math.sqrt(BL...]
    unnamed x9 -> x11, local copies, waits for them, and re-layouts: 6.11 us -> 5.75 us
  transfers between devices with their start and end apart: 1 -> 0, of which waited for: 1 -> 0; matrix products, arithmetic and copies ran while one was open for 0% -> 0% of each run, Pallas kernels for 0% -> 0%
where the time goes in v2:
time: 104 us
  Pallas kernels  97.8 us (94%)
  local copies, waits for them, and re-layouts  5.75 us (6%)
    pallas_call x1, Pallas kernels, shards(): pl.pallas_call(functools.partial(kernel, chips, depth, 1.0 / math.sqrt(BL...  97.8 us
    unnamed x11, local copies, waits for them, and re-layouts  5.75 us

profile of v2, /device:TPU:1, one launch (start us, length us, event | category | flops | bytes accessed | tf_op | source)
XLA Modules:
  0.0 104.2 jit_solution(9950486976186935346)
XLA Ops:
  0.6 0.0 copy-start.1
  0.6 0.6 copy-done.1
  1.3 0.0 copy-start
  1.3 0.8 copy-done
  2.1 97.8 %shard_map.110 = (bf16[128,2048]{1,0:T(8,128)(2,1)S(1)}, bf16[128,2048]{1,0:T(8,128)(2,1)S(1)}, bf16[128,2048]{1,0:T(8,128)(2,1)S(1)}, bf16[128,2048]{1,0:T(8,128)(2,1)}, f32[16,2048]{1,0:T(8,128)S(1)}) custom-call(bf16[128,2048]{1,0:T(8,128)(2,1)} %bitcast.19, bf16[128,2048]{1,0:T(8,128)(2,1)} %bitcast.20, bf16[128,2048]{1,0:T(8,128)(2,1)} %bitcast.21, ...), custom_call_target="tpu_custom_call" | custom-call | tf_op jit(solution)/shard_map/pallas_call | solution.py:592
  99.9 0.8 copy.17
  100.7 0.8 copy.18
  101.5 0.0 copy-start.2
  101.5 0.8 copy.19
  102.3 0.4 copy-done.2
  102.7 0.8 copy.20
  103.5 0.7 copy.21
Async XLA Ops:
  0.6 0.7 copy-start.1
  1.3 0.8 copy-start
  101.5 1.2 %copy-start.2 = (bf16[128,2048]{1,0:T(8,128)(2,1)S(1)}, bf16[128,2048]{1,0:T(8,128)(2,1)}, u32[]{:S(2)}) copy-start(bf16[128,2048]{1,0:T(8,128)(2,1)} %get-tuple-element.13) | copy-start | bytes 1572868

commit v3 on v1

--- a/solution.py
+++ b/solution.py
@@ -10,7 +10,7 @@
 
 BLOCK = 128
 EPSILON = 1e-06
-GROUP = 4
+GROUP = 8
 f32 = jnp.float32
 bf16 = jnp.bfloat16
 MESH = pl.DeviceIdType.MESH
@@ -69,7 +69,7 @@
 
 
 def kernel(
-    chips,
+    chips, depth, scale,
     q_ref, k_ref, v_ref, x_ref, t_ref, w_ref, b_ref,
     o_ref, gq_ref, gk_ref, gv_ref, gw_ref,
     strength, rk_col, rq_col, be_col, rk_row,
@@ -77,7 +77,8 @@
     f_s, f_t, s_t, do_s, e_s, dpq_s, dl_s,
     maps, out_map, chip_map, got_map, prefix, state_out, hand_in, state_in, s_own, s_sib, s_out,
     c_both, c_out, c_chip, c_got, suffix, map_t, grad_out, gh_in, grad_in, g_own, g_sib, g_out,
-    send, recv,
+    gate_out, gate_in, column_out, column_in, depth_out, depth_in, tile_out, tiles,
+    send, recv, gate_send, gate_recv,
 ):
     me = lax.axis_index("seq")
     core = lax.rem(me, 2)
@@ -122,31 +123,23 @@
         def _():
             wait_in(kind, at, dst)
 
+    devices = 2 * chips
+    layer = lax.axis_index("dp")
+
+    def others(count, base, body, first=1):
+        def run(d, carry):
+            body(lax.rem(base + d, count))
+            return carry
+
+        lax.fori_loop(first, count, run, 0)
+
     barrier = pltpu.get_barrier_semaphore()
-
-    def greet(target):
-        @pl.when(target != me)
-        def _():
-            pl.semaphore_signal(barrier, inc=1, device_id={"seq": target}, device_id_type=MESH)
-
-    pl.semaphore_signal(barrier, inc=1, device_id={"seq": sibling}, device_id_type=MESH)
-    for j in range(half):
-        greet(owner(j))
-        greet(source(j))
-
-    logits = mm(x_ref[...], w_ref[...]) + b_ref[...]
+    others(devices, me, lambda t: pl.semaphore_signal(barrier, inc=1, device_id={"seq": t}, device_id_type=MESH))
+    others(depth, layer, lambda t: pl.semaphore_signal(barrier, inc=1, device_id={"dp": t}, device_id_type=MESH))
+
+    logits = mm_rows(x_ref[...], w_ref[...]) + b_ref[...]
     strength[...] = 0.5 / (1.0 + jnp.exp(-logits))
     dl_s[...] = jnp.zeros_like(dl_s)
-
-    own_self = (part == core) & (parity == core)
-
-    @pl.when(own_self)
-    def _():
-        pl.semaphore_wait(barrier, 2 * half - 1)
-
-    @pl.when(jnp.logical_not(own_self))
-    def _():
-        pl.semaphore_wait(barrier, 2 * half + 1)
 
     def span(head):
         return pl.ds(pl.multiple_of(head * BLOCK, BLOCK), BLOCK)
@@ -198,31 +191,26 @@
 
         lax.fori_loop(0, rounds, run, 0)
 
-    def first_other(js):
-        made = local_maps([half + j for j in js], [other_head(j) for j in js])
-        for j, m in zip(js, made):
-            out_map[j] = m
-        for j in js:
-            push(0, j, out_map.at[j], maps.at[core, j], sibling).start()
-
-    steps(first_other)
-
-    def first_own(js):
-        made = local_maps(js, [own_head(j) for j in js])
-        for j, m in zip(js, made):
-            maps[core, j] = m
+    def first(js):
+        slots = [half + j for j in js] + list(js)
+        heads = [other_head(j) for j in js] + [own_head(j) for j in js]
+        made = local_maps(slots, heads)
+        for i, j in enumerate(js):
+            out_map[j] = made[i]
+            maps[core, j] = made[len(js) + i]
+        return slots, heads
+
+    def compose_maps(js):
         for j in js:
             wait_in(0, j, maps.at[1 - core, j])
-        zero = jnp.zeros((BLOCK, BLOCK), f32)
+        nothing = jnp.zeros((BLOCK, BLOCK), f32)
         earlier = [maps[0, j] for j in js]
         later = [maps[1, j] for j in js]
         made = [mm3(b[:, :BLOCK], a) for a, b in zip(earlier, later)]
         for j, m, b in zip(js, made, later):
-            chip_map[j] = m + jnp.concatenate([zero, b[:, BLOCK:]], axis=1)
+            chip_map[j] = m + jnp.concatenate([nothing, b[:, BLOCK:]], axis=1)
         for j in js:
             route(1, j, place, chip_map.at[j], got_map.at[place], owner(j))
-
-    steps(first_own)
 
     def score_terms(slots, heads):
         row, col = masks()
@@ -243,8 +231,15 @@
             z_s[s] = zs[i]
             query_t[s] = queries[i].T
 
-    steps(lambda js: score_terms(js, [own_head(j) for j in js]))
-    steps(lambda js: score_terms([half + j for j in js], [other_head(j) for j in js]))
+    for r in range(2):
+        js = range(r * half // 2, (r + 1) * half // 2)
+        slots, heads = first(js)
+        if r == 0:
+            pl.semaphore_wait(barrier, devices + depth - 2)
+        for j in js:
+            push(0, j, out_map.at[j], maps.at[core, j], sibling).start()
+        score_terms(slots, heads)
+        compose_maps(js)
 
     row, col = masks()
     eyef = (row == col).astype(f32)
@@ -438,44 +433,116 @@
 
     lax.fori_loop(0, half, leave, 0)
 
-    def backward(slots, heads, grads):
+    def gate_terms(slots, heads, grads):
         row, col = masks()
         es = [e_s[s] + mm3(z_s[s], g) for s, g in zip(slots, grads)]
-        gts = [g.T for g in grads]
         efs = [jnp.where(row > col, mm3(e, f_t[s]), 0.0) for e, s in zip(es, slots)]
         ess = [mm3(e, s_t[s]) for e, s in zip(es, slots)]
-        dks = [dpq_s[s] + mm3(f_s[s], gt) for s, gt in zip(slots, gts)]
-        bes = [be_col[s] for s in slots]
-        links = [ef * be for ef, be in zip(efs, bes)]
-        links = [(m + m.T) * rk_row[s] for m, s in zip(links, slots)]
-        dks = [d - es_ * be for d, es_, be in zip(dks, ess, bes)]
-        dks = [d - right_exact(m, k_ref[:, span(h)]) for d, m, h in zip(dks, links, heads)]
         added = 0.0
         lane = lax.broadcasted_iota(jnp.int32, (BLOCK, BLOCK), 1)
+        for i, (s, h) in enumerate(zip(slots, heads)):
+            be = be_col[s]
+            unit = k_ref[:, span(h)].astype(f32) * rk_col[s]
+            gv_ref[:, span(h)] = (es[i] * be).astype(bf16)
+            terms = es[i] * v_ref[:, span(h)].astype(f32) - ess[i] * unit - efs[i] * gram_s[s]
+            dl = jnp.sum(terms, axis=1, keepdims=True) * (be * (1.0 - 2.0 * be))
+            added = added + jnp.where(lane == s, dl, 0.0)
+            p_s[s] = efs[i]
+            p_t[s] = ess[i]
+        dl_s[...] += added
+
+    def key_grads(slots, heads, grads):
+        gts = [g.T for g in grads]
+        bes = [be_col[s] for s in slots]
+        dks = [dpq_s[s] + mm3(f_s[s], gt) for s, gt in zip(slots, gts)]
+        links = [p_s[s] * be for s, be in zip(slots, bes)]
+        links = [(m + m.T) * rk_row[s] for m, s in zip(links, slots)]
+        dks = [d - p_t[s] * be for d, s, be in zip(dks, slots, bes)]
+        dks = [d - right_exact(m, k_ref[:, span(h)]) for d, m, h in zip(dks, links, heads)]
         for i, (s, h) in enumerate(zip(slots, heads)):
             rk = rk_col[s]
             unit = k_ref[:, span(h)].astype(f32) * rk
             grad = rk * (dks[i] - unit * jnp.sum(unit * dks[i], axis=1, keepdims=True))
             gk_ref[:, span(h)] = grad.astype(bf16)
-            gv_ref[:, span(h)] = (es[i] * bes[i]).astype(bf16)
-            terms = es[i] * v_ref[:, span(h)].astype(f32) - ess[i] * unit - efs[i] * gram_s[s]
-            dl = jnp.sum(terms, axis=1, keepdims=True) * (bes[i] * (1.0 - 2.0 * bes[i]))
-            added = added + jnp.where(lane == h, dl, 0.0)
-        dl_s[...] += added
-
-    steps(lambda js: backward(js, [own_head(j) for j in js], [g_own[j] for j in js]))
+
+    side = 2 ** (chips.bit_length() // 2)
+    column, line = lax.div(chip, side), lax.rem(chip, side)
+    start = column * (2 * side)
+    at_row = 2 * line + core
+    in_row = (2 * side, at_row, lambda i: {"seq": start + i})
+    in_column = (chips // side, column, lambda i: {"seq": (i * side + line) * 2 + core})
+    in_depth = (depth, layer, lambda i: {"dp": i})
+
+    def swap(kind, ring, src, dst):
+        count, here, target = ring
+        made = []
+        for d in range(1, count):
+            i = lax.rem(here + d, count)
+            copy = pltpu.make_async_remote_copy(
+                src_ref=src(i), dst_ref=dst.at[here], send_sem=gate_send.at[kind, i],
+                recv_sem=gate_recv.at[kind, here], device_id=target(i), device_id_type=MESH,
+            )
+            copy.start()
+            made.append(copy)
+        return made
+
+    def summed(kind, ring, dst):
+        arrive(kind, ring, dst)
+        total = dst[0]
+        for i in range(1, ring[0]):
+            total = total + dst[i]
+        return total
+
+    def arrive(kind, ring, dst):
+        count, here, target = ring
+        for d in range(1, count):
+            i = lax.rem(here + d, count)
+            pltpu.make_async_remote_copy(
+                src_ref=dst.at[i], dst_ref=dst.at[i], send_sem=gate_send.at[kind, i],
+                recv_sem=gate_recv.at[kind, i], device_id=target(i), device_id_type=MESH,
+            ).wait_recv()
+
+    steps(lambda js: gate_terms(js, [own_head(j) for j in js], [g_own[j] for j in js]))
 
     def last_other(js):
         for j in js:
             wait_in(9, j, g_sib.at[j])
-        backward([half + j for j in js], [other_head(j) for j in js], [g_sib[j] for j in js])
+        gate_terms([half + j for j in js], [other_head(j) for j in js], [g_sib[j] for j in js])
 
     steps(last_other)
 
-    heads = 2 * half
-    gate = dl_s[...].T
-    high, low = split(gate[:heads])
-    gw_ref[...] = mm(high, x_ref[...]) + mm(low, x_ref[...])
+    rows = dl_s[...].T[: 2 * half]
+    parts = jnp.concatenate([rows, rows - rows.astype(bf16).astype(f32)], axis=0).astype(bf16)
+    product = mm(parts, x_ref[...])
+    product = product[: 2 * half] + product[2 * half :]
+    width = gate_out.shape[-1]
+    for y in range(side):
+        gate_out[2 * y + core] = product[:half, y * width : (y + 1) * width]
+        gate_out[2 * y + 1 - core] = product[half:, y * width : (y + 1) * width]
+    gate_in[at_row] = gate_out[at_row]
+    copies = swap(0, in_row, lambda i: gate_out.at[i], gate_in)
+    steps(lambda js: key_grads(js, [own_head(j) for j in js], [g_own[j] for j in js]))
+    total = summed(0, in_row, gate_in)
+    column_out[0] = total
+    column_in[column] = total
+    copies += swap(1, in_column, lambda i: column_out.at[0], column_in)
+    steps(lambda js: key_grads([half + j for j in js], [other_head(j) for j in js], [g_sib[j] for j in js]))
+    total = summed(1, in_column, column_in)
+    depth_out[0] = total
+    depth_in[layer] = total
+    copies += swap(2, in_depth, lambda i: depth_out.at[0], depth_in)
+    total = summed(2, in_depth, depth_in) * scale
+    tile_out[0] = total
+    tiles[at_row] = total
+    copies += swap(3, in_row, lambda i: tile_out.at[0], tiles)
+    arrive(3, in_row, tiles)
+    for t in range(2 * side):
+        tile = tiles[t]
+        for r in range(half):
+            at = 2 * r + t % 2
+            gw_ref[at : at + 1, (t // 2) * width : (t // 2 + 1) * width] = tile[r : r + 1]
+    for copy in copies:
+        copy.wait_send()
 
     def drain(j, carry):
         push(0, j, out_map.at[j], out_map.at[j], sibling).wait_send()
@@ -506,7 +573,15 @@
         push(7, 0, grad_out.at[0], grad_out.at[0], sibling).wait_send()
 
 
-def shards(chips, queries, keys_in, values_in, inputs, target, gate_weight, beta_bias):
+def publish(*refs):
+    copies = [pltpu.make_async_copy(refs[i], refs[5 + i], refs[10].at[i]) for i in range(5)]
+    for copy in copies:
+        copy.start()
+    for copy in copies:
+        copy.wait()
+
+
+def shards(chips, depth, queries, keys_in, values_in, inputs, target, gate_weight, beta_bias):
     heads = gate_weight.shape[1]
     width = heads * BLOCK
     half = heads // 2
@@ -516,6 +591,8 @@
         return pltpu.VMEM((count,) + (tail or square), kind)
 
     wide = (BLOCK, 2 * BLOCK)
+    side = 2 ** (chips.bit_length() // 2)
+    cut = inputs.shape[-1] // side
     scratch = [
         pltpu.VMEM((BLOCK, heads), f32), many(heads, BLOCK, 1), many(heads, BLOCK, 1), many(heads, BLOCK, 1),
         many(heads, 1, BLOCK),
@@ -526,12 +603,15 @@
         many(half + 1, *wide), many(half + 1), many(1), many(half), many(half), many(half), many(half),
         pltpu.VMEM((2, half) + square, f32), many(half), many(half), many(half), many(half + 1), many(half),
         many(half + 1), many(1), many(half), many(half), many(half), many(half),
+        many(2 * side, half, cut), many(2 * side, half, cut), many(1, half, cut), many(chips // side, half, cut),
+        many(1, half, cut), many(depth, half, cut), many(1, half, cut), many(2 * side, half, cut),
         pltpu.SemaphoreType.DMA((10, half)), pltpu.SemaphoreType.DMA((10, half)),
+        pltpu.SemaphoreType.DMA((4, 16)), pltpu.SemaphoreType.DMA((4, 16)),
     ]
     rows = jax.ShapeDtypeStruct((BLOCK, width), bf16)
     whole = pl.BlockSpec(memory_space=pltpu.VMEM)
     results = pl.pallas_call(
-        functools.partial(kernel, chips),
+        functools.partial(kernel, chips, depth, 1.0 / math.sqrt(BLOCK * 2 * chips * depth)),
         out_shape=(rows, rows, rows, rows, jax.ShapeDtypeStruct((heads, inputs.shape[-1]), f32)),
         in_specs=[whole] * 7,
         out_specs=(whole,) * 5,
@@ -539,19 +619,24 @@
         compiler_params=pltpu.CompilerParams(
             collective_id=0, has_side_effects=True, vmem_limit_bytes=52 * 1024 * 1024
         ),
-    )(queries[0], keys_in[0], values_in[0], inputs[0], target[0], gate_weight, beta_bias[None])
-    output, grad_q, grad_k, grad_v, local_weight = results
-    total = lax.psum(local_weight, ("seq", "dp"))
-    tokens = BLOCK * lax.axis_size("seq") * lax.axis_size("dp")
-    scaled = total.T * (1.0 / math.sqrt(tokens))
-    return (output[None], grad_q[None], grad_k[None], grad_v[None], scaled)
+    )(queries[0], keys_in[0], values_in[0], inputs[0], target[0], gate_weight.T, beta_bias[None])
+    anywhere = pl.BlockSpec(memory_space=pl.ANY)
+    output, grad_q, grad_k, grad_v, grad_w = pl.pallas_call(
+        publish,
+        out_shape=tuple(jax.ShapeDtypeStruct(r.shape, r.dtype) for r in results),
+        in_specs=[anywhere] * 5,
+        out_specs=(anywhere,) * 5,
+        scratch_shapes=[pltpu.SemaphoreType.DMA((5,))],
+        compiler_params=pltpu.CompilerParams(vmem_limit_bytes=1024 * 1024),
+    )(*results)
+    return (output[None], grad_q[None], grad_k[None], grad_v[None], grad_w.T)
 
 
 def solution(mesh):
     placed = P("dp", "seq", None)
     chips = mesh.shape["seq"] // 2
     return jax.shard_map(
-        functools.partial(shards, chips),
+        functools.partial(shards, chips, mesh.shape["dp"]),
         mesh=mesh,
         in_specs=(placed,) * 5 + (P(), P()),
         out_specs=(placed,) * 4 + (P(),),

time: 242 us -> 96.2 us (0.40)
  waiting for transfers between devices: 140 us -> 0 us
  between operations: 14 us -> 0.82 us
  Pallas kernels: 80.3 us -> 92.7 us
  local copies, waits for them, and re-layouts: 6.11 us -> 2.52 us
    psum x1 -> x0, waiting for transfers between devices: 140 us -> none  [shards(): total = lax.psum(local_weight, ('seq', 'dp'))]
    pallas_call x1 -> x2, Pallas kernels: 80.3 us -> 92.7 us  [the longest x1 91.3 us: shards(): pl.pallas_call(functools.partial(kernel, chips, depth, 1.0 / math.sqrt(BL...]
    unnamed x9 -> x6, local copies, waits for them, and re-layouts: 6.11 us -> 2.52 us
  transfers between devices with their start and end apart: 1 -> 0, of which waited for: 1 -> 0; matrix products, arithmetic and copies ran while one was open for 0% -> 0% of each run, Pallas kernels for 0% -> 0%
where the time goes in v3:
time: 96.2 us; the launch traced here: 96 us
  Pallas kernels  92.7 us (96%)
  local copies, waits for them, and re-layouts  2.52 us (3%)
    pallas_call x1, Pallas kernels, shards(): pl.pallas_call(functools.partial(kernel, chips, depth, 1.0 / math.sqrt(BL...  91.3 us
    unnamed x6, local copies, waits for them, and re-layouts  2.52 us

profile of v3, /device:TPU:1, one launch (start us, length us, event | category | flops | bytes accessed | tf_op | source)
XLA Modules:
  0.0 96.0 jit_solution(13260790677901746871)
XLA Ops:
  0.6 0.0 copy-start.2
  0.6 0.6 copy-done.2
  1.3 0.0 copy-start.1
  1.3 0.8 copy-done.1
  2.1 91.3 %shard_map.110 = (bf16[128,2048]{1,0:T(8,128)(2,1)S(1)}, bf16[128,2048]{1,0:T(8,128)(2,1)S(1)}, bf16[128,2048]{1,0:T(8,128)(2,1)S(1)}, bf16[128,2048]{1,0:T(8,128)(2,1)}, f32[16,2048]{1,0:T(8,128)S(1)}) custom-call(bf16[128,2048]{1,0:T(8,128)(2,1)} %bitcast.14, bf16[128,2048]{1,0:T(8,128)(2,1)} %bitcast.15, bf16[128,2048]{1,0:T(8,128)(2,1)} %bitcast.16, ...), custom_call_target="tpu_custom_call" | custom-call | tf_op jit(solution)/shard_map/pallas_call | solution.py:613
  93.4 0.0 copy-start
  93.4 1.0 %copy-done = bf16[128,2048]{1,0:T(8,128)(2,1)S(1)} copy-done((bf16[128,2048]{1,0:T(8,128)(2,1)S(1)}, bf16[128,2048]{1,0:T(8,128)(2,1)}, u32[]{:S(2)}) %copy-start) | copy-done | bytes 524312
  94.4 1.4 %shard_map.111 = (bf16[128,2048]{1,0:T(8,128)(2,1)}, bf16[128,2048]{1,0:T(8,128)(2,1)}, bf16[128,2048]{1,0:T(8,128)(2,1)}, bf16[128,2048]{1,0:T(8,128)(2,1)}, f32[16,2048]{1,0:T(8,128)}) custom-call(bf16[128,2048]{1,0:T(8,128)(2,1)S(1)} %get-tuple-element.15.refs_0_, bf16[128,2048]{1,0:T(8,128)(2,1)S(1)} %get-tuple-element.16.refs_1_, ...), custom_call_target="tpu_custom_call" | custom-call | tf_op jit(solution)/shard_map/pallas_call | solution.py:624
Async XLA Ops:
  0.6 0.7 copy-start.2
  1.3 0.8 copy-start.1
  93.4 1.0 %copy-start = (bf16[128,2048]{1,0:T(8,128)(2,1)S(1)}, bf16[128,2048]{1,0:T(8,128)(2,1)}, u32[]{:S(2)}) copy-start(bf16[128,2048]{1,0:T(8,128)(2,1)} %get-tuple-element.18.refs_3_) | copy-start | bytes 1572868

commit v4 on v3

--- a/solution.py
+++ b/solution.py
@@ -74,7 +74,7 @@
     o_ref, gq_ref, gk_ref, gv_ref, gw_ref,
     strength, rk_col, rq_col, be_col, rk_row,
     key_t, query_t, gram_s, inv_s, inv_t, wk_s, wv_s, p_s, p_t, z_s,
-    f_s, f_t, s_t, do_s, e_s, dpq_s, dl_s,
+    early_t, late_t, f_s, f_t, s_t, do_s, e_s, dpq_s, dl_s,
     maps, out_map, chip_map, got_map, prefix, state_out, hand_in, state_in, s_own, s_sib, s_out,
     c_both, c_out, c_chip, c_got, suffix, map_t, grad_out, gh_in, grad_in, g_own, g_sib, g_out,
     gate_out, gate_in, column_out, column_in, depth_out, depth_in, tile_out, tiles,
@@ -86,13 +86,21 @@
     half = chips // 2
     part = lax.div(chip, half)
     place = lax.rem(chip, half)
-    parity = lax.rem(chip, 2)
+    across, along = lax.div(chip, 4), lax.rem(chip, 4)
+    spread = chips == 16
+    mine = 8 * lax.rem(across + along, 2) + 2 * across + lax.div(along, 2) if spread else chip
+    parity = lax.rem(mine, 2)
     sibling = me + 1 - 2 * core
     rounds = half // min(GROUP, half)
     group = min(GROUP, half)
 
     def owner(j):
-        return 2 * (2 * j + core) + part
+        head = 2 * j + core
+        if spread:
+            bank, seat = lax.div(head, 8), lax.rem(head, 8)
+            line = lax.div(seat, 2)
+            head = 4 * line + 2 * lax.rem(seat, 2) + lax.rem(line + bank, 2)
+        return 2 * head + part
 
     def source(i):
         return 2 * (half * core + i) + parity
@@ -184,13 +192,6 @@
         eyef = eye.astype(f32)
         return [jnp.concatenate([eyef - m[:, :BLOCK], m[:, BLOCK:]], axis=1) for m in both]
 
-    def steps(body):
-        def run(r, carry):
-            body([r * group + u for u in range(group)])
-            return carry
-
-        lax.fori_loop(0, rounds, run, 0)
-
     def first(js):
         slots = [half + j for j in js] + list(js)
         heads = [other_head(j) for j in js] + [own_head(j) for j in js]
@@ -245,7 +246,7 @@
     eyef = (row == col).astype(f32)
     zero = jnp.zeros((BLOCK, BLOCK), f32)
 
-    slot = lax.div(chip, 2)
+    slot = lax.div(mine, 2)
 
     @pl.when(core == 0)
     def _():
@@ -298,17 +299,21 @@
 
         lax.fori_loop(0, rounds, lift, 0)
 
-    def enter(j, carry):
-        routed(3, j, state_in.at[j], owner(j))
-        first = state_in[j]
-        step = maps[0, j]
-        second = mm3(step[:, :BLOCK], first) + step[:, BLOCK:]
-        s_own[j] = jnp.where(core == 0, first, second)
-        s_out[j] = jnp.where(core == 0, second, first)
-        push(4, j, s_out.at[j], s_sib.at[j], sibling).start()
-        return carry
-
-    lax.fori_loop(0, half, enter, 0)
+    for j in range(half):
+        early_t[j] = maps[0, j][:, :BLOCK].T
+        late_t[j] = maps[1, j][:, :BLOCK].T
+
+    def enter(js):
+        for j in js:
+            routed(3, j, state_in.at[j], owner(j))
+        firsts = [state_in[j] for j in js]
+        steps_ = [maps[0, j] for j in js]
+        seconds = [mm3(m[:, :BLOCK], a) + m[:, BLOCK:] for m, a in zip(steps_, firsts)]
+        for j, a, b in zip(js, firsts, seconds):
+            s_own[j] = jnp.where(core == 0, a, b)
+            s_out[j] = jnp.where(core == 0, b, a)
+        for j in js:
+            push(4, j, s_out.at[j], s_sib.at[j], sibling).start()
 
     def forward(slots, heads, states):
         queries = [q_ref[:, span(h)] for h in heads]
@@ -329,34 +334,14 @@
             e_s[s] = es[i]
         return cs
 
-    def second_own(js):
-        made = forward(js, [own_head(j) for j in js], [s_own[j] for j in js])
-        for j, c in zip(js, made):
-            c_both[core, j] = c
-
-    steps(second_own)
-
-    def second_other(js):
-        for j in js:
-            wait_in(4, j, s_sib.at[j])
-        made = forward([half + j for j in js], [other_head(j) for j in js], [s_sib[j] for j in js])
-        for j, c in zip(js, made):
-            c_out[j] = c
-        for j in js:
-            push(5, j, c_out.at[j], c_both.at[core, j], sibling).start()
-
-    steps(second_other)
-
     def join_grads(js):
         for j in js:
             wait_in(5, j, c_both.at[1 - core, j])
-        made = [mm3(maps[0, j][:, :BLOCK].T, c_both[1, j]) + c_both[0, j] for j in js]
+        made = [mm3(early_t[j], c_both[1, j]) + c_both[0, j] for j in js]
         for j, c in zip(js, made):
             c_chip[j] = c
         for j in js:
             route(6, j, place, c_chip.at[j], c_got.at[place], owner(j))
-
-    steps(join_grads)
 
     def query_grads(slots, heads, states):
         row, col = masks()
@@ -378,12 +363,45 @@
             f_t[s] = fts[i]
             s_t[s] = sts[i]
 
-    steps(lambda js: query_grads(js, [own_head(j) for j in js], [s_own[j] for j in js]))
-    steps(
-        lambda js: query_grads(
-            [half + j for j in js], [other_head(j) for j in js], [s_sib[j] for j in js]
-        )
-    )
+    def both(body, js, ours, theirs):
+        slots = list(js) + [half + j for j in js]
+        heads = [own_head(j) for j in js] + [other_head(j) for j in js]
+        return body(slots, heads, [ours[j] for j in js] + [theirs[j] for j in js])
+
+    for r in range(2):
+        js = range(r * half // 2, (r + 1) * half // 2)
+        enter(js)
+        for j in js:
+            wait_in(4, j, s_sib.at[j])
+        made = both(forward, js, s_own, s_sib)
+        for i, j in enumerate(js):
+            c_both[core, j] = made[i]
+            c_out[j] = made[len(js) + i]
+        for j in js:
+            push(5, j, c_out.at[j], c_both.at[core, j], sibling).start()
+        if r == 0:
+            both(query_grads, js, s_own, s_sib)
+        join_grads(js)
+    both(query_grads, js, s_own, s_sib)
+
+    def drain_early(j, carry):
+        push(0, j, out_map.at[j], out_map.at[j], sibling).wait_send()
+        push(4, j, s_out.at[j], s_out.at[j], sibling).wait_send()
+        push(5, j, c_out.at[j], c_out.at[j], sibling).wait_send()
+
+        @pl.when(owner(j) != me)
+        def _():
+            push(1, j, chip_map.at[j], chip_map.at[j], sibling).wait_send()
+
+        @pl.when(source(j) != me)
+        def _():
+            push(3, j, state_out.at[j], state_out.at[j], sibling).wait_send()
+
+        return carry
+
+    @pl.when(core == 0)
+    def _():
+        push(2, 0, state_out.at[half], state_out.at[half], sibling).wait_send()
 
     grad_out[half] = zero
 
@@ -422,16 +440,18 @@
 
         lax.fori_loop(0, rounds, lift, 0)
 
-    def leave(j, carry):
-        routed(8, j, grad_in.at[j], owner(j))
-        last = grad_in[j]
-        inner = mm3(maps[1, j][:, :BLOCK].T, last) + c_both[1, j]
-        g_own[j] = jnp.where(core == 0, inner, last)
-        g_out[j] = jnp.where(core == 0, last, inner)
-        push(9, j, g_out.at[j], g_sib.at[j], sibling).start()
-        return carry
-
-    lax.fori_loop(0, half, leave, 0)
+    lax.fori_loop(0, half, drain_early, 0)
+
+    def leave(js):
+        for j in js:
+            routed(8, j, grad_in.at[j], owner(j))
+        lasts = [grad_in[j] for j in js]
+        inners = [mm3(late_t[j], g) + c_both[1, j] for j, g in zip(js, lasts)]
+        for j, a, b in zip(js, lasts, inners):
+            g_own[j] = jnp.where(core == 0, b, a)
+            g_out[j] = jnp.where(core == 0, a, b)
+        for j in js:
+            push(9, j, g_out.at[j], g_sib.at[j], sibling).start()
 
     def gate_terms(slots, heads, grads):
         row, col = masks()
@@ -502,14 +522,12 @@
                 recv_sem=gate_recv.at[kind, i], device_id=target(i), device_id_type=MESH,
             ).wait_recv()
 
-    steps(lambda js: gate_terms(js, [own_head(j) for j in js], [g_own[j] for j in js]))
-
-    def last_other(js):
+    for r in range(2):
+        js = range(r * half // 2, (r + 1) * half // 2)
+        leave(js)
         for j in js:
             wait_in(9, j, g_sib.at[j])
-        gate_terms([half + j for j in js], [other_head(j) for j in js], [g_sib[j] for j in js])
-
-    steps(last_other)
+        both(gate_terms, js, g_own, g_sib)
 
     rows = dl_s[...].T[: 2 * half]
     parts = jnp.concatenate([rows, rows - rows.astype(bf16).astype(f32)], axis=0).astype(bf16)
@@ -521,56 +539,50 @@
         gate_out[2 * y + 1 - core] = product[half:, y * width : (y + 1) * width]
     gate_in[at_row] = gate_out[at_row]
     copies = swap(0, in_row, lambda i: gate_out.at[i], gate_in)
-    steps(lambda js: key_grads(js, [own_head(j) for j in js], [g_own[j] for j in js]))
+    both(key_grads, range(half // 2), g_own, g_sib)
     total = summed(0, in_row, gate_in)
     column_out[0] = total
     column_in[column] = total
     copies += swap(1, in_column, lambda i: column_out.at[0], column_in)
-    steps(lambda js: key_grads([half + j for j in js], [other_head(j) for j in js], [g_sib[j] for j in js]))
+    both(key_grads, range(half // 2, half), g_own, g_sib)
     total = summed(1, in_column, column_in)
     depth_out[0] = total
     depth_in[layer] = total
     copies += swap(2, in_depth, lambda i: depth_out.at[0], depth_in)
+
+    def drain_late(j, carry):
+        push(9, j, g_out.at[j], g_out.at[j], sibling).wait_send()
+
+        @pl.when(owner(j) != me)
+        def _():
+            push(6, j, c_chip.at[j], c_chip.at[j], sibling).wait_send()
+
+        @pl.when(source(j) != me)
+        def _():
+            push(8, j, grad_out.at[j + 1], grad_out.at[j + 1], sibling).wait_send()
+
+        return carry
+
+    lax.fori_loop(0, half, drain_late, 0)
+
+    @pl.when(core == 1)
+    def _():
+        push(7, 0, grad_out.at[0], grad_out.at[0], sibling).wait_send()
+
     total = summed(2, in_depth, depth_in) * scale
     tile_out[0] = total
     tiles[at_row] = total
-    copies += swap(3, in_row, lambda i: tile_out.at[0], tiles)
+    last = swap(3, in_row, lambda i: tile_out.at[0], tiles)
+    for copy in copies:
+        copy.wait_send()
     arrive(3, in_row, tiles)
     for t in range(2 * side):
         tile = tiles[t]
         for r in range(half):
             at = 2 * r + t % 2
             gw_ref[at : at + 1, (t // 2) * width : (t // 2 + 1) * width] = tile[r : r + 1]
-    for copy in copies:
+    for copy in last:
         copy.wait_send()
-
-    def drain(j, carry):
-        push(0, j, out_map.at[j], out_map.at[j], sibling).wait_send()
-        push(4, j, s_out.at[j], s_out.at[j], sibling).wait_send()
-        push(5, j, c_out.at[j], c_out.at[j], sibling).wait_send()
-        push(9, j, g_out.at[j], g_out.at[j], sibling).wait_send()
-
-        @pl.when(owner(j) != me)
-        def _():
-            push(1, j, chip_map.at[j], chip_map.at[j], sibling).wait_send()
-            push(6, j, c_chip.at[j], c_chip.at[j], sibling).wait_send()
-
-        @pl.when(source(j) != me)
-        def _():
-            push(3, j, state_out.at[j], state_out.at[j], sibling).wait_send()
-            push(8, j, grad_out.at[j + 1], grad_out.at[j + 1], sibling).wait_send()
-
-        return carry
-
-    lax.fori_loop(0, half, drain, 0)
-
-    @pl.when(core == 0)
-    def _():
-        push(2, 0, state_out.at[half], state_out.at[half], sibling).wait_send()
-
-    @pl.when(core == 1)
-    def _():
-        push(7, 0, grad_out.at[0], grad_out.at[0], sibling).wait_send()
 
 
 def publish(*refs):
@@ -597,7 +609,7 @@
         pltpu.VMEM((BLOCK, heads), f32), many(heads, BLOCK, 1), many(heads, BLOCK, 1), many(heads, BLOCK, 1),
         many(heads, 1, BLOCK),
         many(heads, kind=bf16), many(heads, kind=bf16),
-    ] + [many(heads)] * 8 + [many(heads)] * 6 + [
+    ] + [many(heads)] * 8 + [many(half)] * 2 + [many(heads)] * 6 + [
         pltpu.VMEM(square, f32),
         pltpu.VMEM((2, half) + wide, f32), many(half, *wide), many(half, *wide), many(half, *wide),
         many(half + 1, *wide), many(half + 1), many(1), many(half), many(half), many(half), many(half),

time: 96.2 us -> 95.4 us (level)
  no operation moved by 1% of the time
where the time goes in v4:
time: 95.4 us; the launch traced here: 95.2 us
  Pallas kernels  91.8 us (96%)
  local copies, waits for them, and re-layouts  2.52 us (3%)
    pallas_call x1, Pallas kernels, shards(): pl.pallas_call(functools.partial(kernel, chips, depth, 1.0 / math.sqrt(BL...  90.4 us
    unnamed x6, local copies, waits for them, and re-layouts  2.52 us

profile of v4, /device:TPU:1, one launch (start us, length us, event | category | flops | bytes accessed | tf_op | source)
XLA Modules:
  0.0 95.2 jit_solution(13071940831661601915)
XLA Ops:
  0.6 0.0 copy-start.2
  0.6 0.6 copy-done.2
  1.3 0.0 copy-start.1
  1.3 0.8 copy-done.1
  2.1 90.4 %shard_map.110 = (bf16[128,2048]{1,0:T(8,128)(2,1)S(1)}, bf16[128,2048]{1,0:T(8,128)(2,1)S(1)}, bf16[128,2048]{1,0:T(8,128)(2,1)S(1)}, bf16[128,2048]{1,0:T(8,128)(2,1)}, f32[16,2048]{1,0:T(8,128)S(1)}) custom-call(bf16[128,2048]{1,0:T(8,128)(2,1)} %bitcast.14, bf16[128,2048]{1,0:T(8,128)(2,1)} %bitcast.15, bf16[128,2048]{1,0:T(8,128)(2,1)} %bitcast.16, ...), custom_call_target="tpu_custom_call" | custom-call | tf_op jit(solution)/shard_map/pallas_call | solution.py:625
  92.6 0.0 copy-start
  92.6 1.0 %copy-done = bf16[128,2048]{1,0:T(8,128)(2,1)S(1)} copy-done((bf16[128,2048]{1,0:T(8,128)(2,1)S(1)}, bf16[128,2048]{1,0:T(8,128)(2,1)}, u32[]{:S(2)}) %copy-start) | copy-done | bytes 524312
  93.6 1.4 %shard_map.111 = (bf16[128,2048]{1,0:T(8,128)(2,1)}, bf16[128,2048]{1,0:T(8,128)(2,1)}, bf16[128,2048]{1,0:T(8,128)(2,1)}, bf16[128,2048]{1,0:T(8,128)(2,1)}, f32[16,2048]{1,0:T(8,128)}) custom-call(bf16[128,2048]{1,0:T(8,128)(2,1)S(1)} %get-tuple-element.15.refs_0_, bf16[128,2048]{1,0:T(8,128)(2,1)S(1)} %get-tuple-element.16.refs_1_, ...), custom_call_target="tpu_custom_call" | custom-call | tf_op jit(solution)/shard_map/pallas_call | solution.py:636
Async XLA Ops:
  0.6 0.7 copy-start.2
  1.3 0.8 copy-start.1
  92.6 1.0 %copy-start = (bf16[128,2048]{1,0:T(8,128)(2,1)S(1)}, bf16[128,2048]{1,0:T(8,128)(2,1)}, u32[]{:S(2)}) copy-start(bf16[128,2048]{1,0:T(8,128)(2,1)} %get-tuple-element.18.refs_3_) | copy-start | bytes 1572868

commit v5 on v4

--- a/solution.py
+++ b/solution.py
@@ -26,6 +26,10 @@
 
 def mm3(a, b):
     return jnp.dot(a, b, preferred_element_type=f32, precision=lax.Precision.HIGH)
+
+
+def mm3_rows(a, b):
+    return lax.dot_general(a, b, (((1,), (1,)), ((), ())), preferred_element_type=f32, precision=lax.Precision.HIGH)
 
 
 def split(x):
@@ -251,15 +255,20 @@
     @pl.when(core == 0)
     def _():
         state_out[0] = zero
-
-        def lap(i, carry):
-            routed(1, i, got_map.at[i], source(i))
-            route(3, i, slot, state_out.at[i], state_in.at[slot], source(i))
-            step = got_map[i]
-            state_out[i + 1] = mm3(step[:, :BLOCK], state_out[i]) + step[:, BLOCK:]
-            return carry
-
-        lax.fori_loop(0, half, lap, 0)
+        turned_state = None
+        for r in range(2):
+            here = range(r * half // 2, (r + 1) * half // 2)
+            for i in here:
+                routed(1, i, got_map.at[i], source(i))
+            for i in here:
+                step = got_map[i]
+                if turned_state is None:
+                    turned_state = step[:, BLOCK:].T
+                else:
+                    turned_state = mm3_rows(turned_state, step[:, :BLOCK]) + step[:, BLOCK:].T
+                state_out[i + 1] = turned_state.T
+            for i in here:
+                route(3, i, slot, state_out.at[i], state_in.at[slot], source(i))
         push(2, 0, state_out.at[half], hand_in.at[0], sibling).start()
         suffix[half] = eyef
 
@@ -407,14 +416,19 @@
 
     @pl.when(core == 1)
     def _():
-        def lap(n, carry):
-            i = half - 1 - n
-            routed(6, i, c_got.at[i], source(i))
-            route(8, i, slot, grad_out.at[i + 1], grad_in.at[slot], source(i))
-            grad_out[i] = mm3(map_t[i], grad_out[i + 1]) + c_got[i]
-            return carry
-
-        lax.fori_loop(0, half, lap, 0)
+        turned_grad = None
+        for r in range(2):
+            here = [half - 1 - i for i in range(r * half // 2, (r + 1) * half // 2)]
+            for i in here:
+                routed(6, i, c_got.at[i], source(i))
+            for i in here:
+                if turned_grad is None:
+                    turned_grad = c_got[i].T
+                else:
+                    turned_grad = mm3(turned_grad, got_map[i][:, :BLOCK]) + c_got[i].T
+                grad_out[i] = turned_grad.T
+            for i in here:
+                route(8, i, slot, grad_out.at[i + 1], grad_in.at[slot], source(i))
         push(7, 0, grad_out.at[0], gh_in.at[0], sibling).start()
 
     @pl.when(core == 0)
@@ -629,7 +643,7 @@
         out_specs=(whole,) * 5,
         scratch_shapes=scratch,
         compiler_params=pltpu.CompilerParams(
-            collective_id=0, has_side_effects=True, vmem_limit_bytes=52 * 1024 * 1024
+            collective_id=0, has_side_effects=True, vmem_limit_bytes=49 * 1024 * 1024
         ),
     )(queries[0], keys_in[0], values_in[0], inputs[0], target[0], gate_weight.T, beta_bias[None])
     anywhere = pl.BlockSpec(memory_space=pl.ANY)

time: 95.4 us -> 94.5 us (level)
  Pallas kernels: 91.8 us -> 86.5 us
  local copies, waits for them, and re-layouts: 2.52 us -> 6.69 us
    pallas_call x1, Pallas kernels: 90.4 us -> 85.2 us  [shards(): pl.pallas_call(functools.partial(kernel, chips, depth, 1.0 / math.sqrt(BL...]
    unnamed x6 -> x14, local copies, waits for them, and re-layouts: 2.52 us -> 6.69 us
where the time goes in v5:
time: 94.5 us; the launch traced here: 94.1 us
  Pallas kernels  86.5 us (92%)
  local copies, waits for them, and re-layouts  6.69 us (7%)
    pallas_call x1, Pallas kernels, shards(): pl.pallas_call(functools.partial(kernel, chips, depth, 1.0 / math.sqrt(BL...  85.2 us
    unnamed x14, local copies, waits for them, and re-layouts  6.69 us

profile of v5, /device:TPU:1, one launch (start us, length us, event | category | flops | bytes accessed | tf_op | source)
XLA Modules:
  0.0 94.1 jit_solution(12612679210623020248)
XLA Ops:
  0.6 0.0 copy-start.6
  0.6 0.6 copy-done.6
  1.3 0.0 copy-start
  1.3 1.0 %copy-done = bf16[1,128,2048]{2,1,0:T(8,128)(2,1)S(1)} copy-done((bf16[1,128,2048]{2,1,0:T(8,128)(2,1)S(1)}, bf16[1,128,2048]{2,1,0:T(8,128)(2,1)}, u32[]{:S(2)}) %copy-start) | copy-done | bytes 524312
  2.3 0.0 copy-start.1
  2.3 1.0 %copy-done.1 = bf16[1,128,2048]{2,1,0:T(8,128)(2,1)S(1)} copy-done((bf16[1,128,2048]{2,1,0:T(8,128)(2,1)S(1)}, bf16[1,128,2048]{2,1,0:T(8,128)(2,1)}, u32[]{:S(2)}) %copy-start.1) | copy-done | bytes 524312
  3.4 0.0 copy-start.2
  3.4 1.0 %copy-done.2 = bf16[1,128,2048]{2,1,0:T(8,128)(2,1)S(1)} copy-done((bf16[1,128,2048]{2,1,0:T(8,128)(2,1)S(1)}, bf16[1,128,2048]{2,1,0:T(8,128)(2,1)}, u32[]{:S(2)}) %copy-start.2) | copy-done | bytes 524312
  4.4 0.0 copy-start.3
  4.4 1.0 %copy-done.3 = bf16[1,128,2048]{2,1,0:T(8,128)(2,1)S(1)} copy-done((bf16[1,128,2048]{2,1,0:T(8,128)(2,1)S(1)}, bf16[1,128,2048]{2,1,0:T(8,128)(2,1)}, u32[]{:S(2)}) %copy-start.3) | copy-done | bytes 524312
  5.5 0.0 copy-start.4
  5.5 1.0 %copy-done.4 = bf16[1,128,2048]{2,1,0:T(8,128)(2,1)S(1)} copy-done((bf16[1,128,2048]{2,1,0:T(8,128)(2,1)S(1)}, bf16[1,128,2048]{2,1,0:T(8,128)(2,1)}, u32[]{:S(2)}) %copy-start.4) | copy-done | bytes 524312
  6.5 0.0 copy-start.5
  6.5 0.8 copy-done.5
  7.3 85.2 %shard_map.110 = (bf16[128,2048]{1,0:T(8,128)(2,1)S(1)}, bf16[128,2048]{1,0:T(8,128)(2,1)S(1)}, bf16[128,2048]{1,0:T(8,128)(2,1)S(1)}, bf16[128,2048]{1,0:T(8,128)(2,1)S(1)}, f32[16,2048]{1,0:T(8,128)S(1)}) custom-call(bf16[128,2048]{1,0:T(8,128)(2,1)S(1)} %bitcast.12, bf16[128,2048]{1,0:T(8,128)(2,1)S(1)} %bitcast.13, bf16[128,2048]{1,0:T(8,128)(2,1)S(1)} %bitcast.14, ...), custom_call_target="tpu_custom_call" | custom-call | tf_op jit(solution)/shard_map/pallas_call | solution.py:639
  92.5 1.4 %shard_map.111 = (bf16[128,2048]{1,0:T(8,128)(2,1)}, bf16[128,2048]{1,0:T(8,128)(2,1)}, bf16[128,2048]{1,0:T(8,128)(2,1)}, bf16[128,2048]{1,0:T(8,128)(2,1)}, f32[16,2048]{1,0:T(8,128)}) custom-call(bf16[128,2048]{1,0:T(8,128)(2,1)S(1)} %get-tuple-element.15.refs_0_, bf16[128,2048]{1,0:T(8,128)(2,1)S(1)} %get-tuple-element.16.refs_1_, ...), custom_call_target="tpu_custom_call" | custom-call | tf_op jit(solution)/shard_map/pallas_call | solution.py:650
Async XLA Ops:
  0.6 0.7 copy-start.6
  1.3 1.0 %copy-start = (bf16[1,128,2048]{2,1,0:T(8,128)(2,1)S(1)}, bf16[1,128,2048]{2,1,0:T(8,128)(2,1)}, u32[]{:S(2)}) copy-start(bf16[1,128,2048]{2,1,0:T(8,128)(2,1)} %param.7) | copy-start | bytes 1572868
  2.3 1.0 %copy-start.1 = (bf16[1,128,2048]{2,1,0:T(8,128)(2,1)S(1)}, bf16[1,128,2048]{2,1,0:T(8,128)(2,1)}, u32[]{:S(2)}) copy-start(bf16[1,128,2048]{2,1,0:T(8,128)(2,1)} %param.8) | copy-start | bytes 1572868
  3.4 1.0 %copy-start.2 = (bf16[1,128,2048]{2,1,0:T(8,128)(2,1)S(1)}, bf16[1,128,2048]{2,1,0:T(8,128)(2,1)}, u32[]{:S(2)}) copy-start(bf16[1,128,2048]{2,1,0:T(8,128)(2,1)} %param.9) | copy-start | bytes 1572868
  4.4 1.0 %copy-start.3 = (bf16[1,128,2048]{2,1,0:T(8,128)(2,1)S(1)}, bf16[1,128,2048]{2,1,0:T(8,128)(2,1)}, u32[]{:S(2)}) copy-start(bf16[1,128,2048]{2,1,0:T(8,128)(2,1)} %param.10) | copy-start | bytes 1572868
  5.5 1.0 %copy-start.4 = (bf16[1,128,2048]{2,1,0:T(8,128)(2,1)S(1)}, bf16[1,128,2048]{2,1,0:T(8,128)(2,1)}, u32[]{:S(2)}) copy-start(bf16[1,128,2048]{2,1,0:T(8,128)(2,1)} %param.11) | copy-start | bytes 1572868
  6.5 0.8 copy-start.5

commit v6 on v5

--- a/solution.py
+++ b/solution.py
@@ -643,7 +643,7 @@
         out_specs=(whole,) * 5,
         scratch_shapes=scratch,
         compiler_params=pltpu.CompilerParams(
-            collective_id=0, has_side_effects=True, vmem_limit_bytes=49 * 1024 * 1024
+            collective_id=0, has_side_effects=True, vmem_limit_bytes=51 * 1024 * 1024
         ),
     )(queries[0], keys_in[0], values_in[0], inputs[0], target[0], gate_weight.T, beta_bias[None])
     anywhere = pl.BlockSpec(memory_space=pl.ANY)

time: 94.5 us -> 93.8 us (level)
  local copies, waits for them, and re-layouts: 6.69 us -> 2.53 us
  Pallas kernels: 86.5 us -> 90.2 us
    unnamed x14 -> x6, local copies, waits for them, and re-layouts: 6.69 us -> 2.53 us
    pallas_call x1, Pallas kernels: 85.2 us -> 88.8 us  [shards(): pl.pallas_call(functools.partial(kernel, chips, depth, 1.0 / math.sqrt(BL...]
where the time goes in v6:
time: 93.8 us; the launch traced here: 93.6 us
  Pallas kernels  90.2 us (96%)
  local copies, waits for them, and re-layouts  2.53 us (3%)
    pallas_call x1, Pallas kernels, shards(): pl.pallas_call(functools.partial(kernel, chips, depth, 1.0 / math.sqrt(BL...  88.8 us
    unnamed x6, local copies, waits for them, and re-layouts  2.53 us

profile of v6, /device:TPU:1, one launch (start us, length us, event | category | flops | bytes accessed | tf_op | source)
XLA Modules:
  0.0 93.6 jit_solution(5285418544840217883)
XLA Ops:
  0.6 0.0 copy-start.2
  0.6 0.6 copy-done.2
  1.3 0.0 copy-start
  1.3 1.0 %copy-done = bf16[1,128,2048]{2,1,0:T(8,128)(2,1)S(1)} copy-done((bf16[1,128,2048]{2,1,0:T(8,128)(2,1)S(1)}, bf16[1,128,2048]{2,1,0:T(8,128)(2,1)}, u32[]{:S(2)}) %copy-start) | copy-done | bytes 524312
  2.3 0.0 copy-start.1
  2.3 0.8 copy-done.1
  3.2 88.8 %shard_map.110 = (bf16[128,2048]{1,0:T(8,128)(2,1)S(1)}, bf16[128,2048]{1,0:T(8,128)(2,1)S(1)}, bf16[128,2048]{1,0:T(8,128)(2,1)S(1)}, bf16[128,2048]{1,0:T(8,128)(2,1)S(1)}, f32[16,2048]{1,0:T(8,128)S(1)}) custom-call(bf16[128,2048]{1,0:T(8,128)(2,1)S(1)} %bitcast.12, bf16[128,2048]{1,0:T(8,128)(2,1)} %bitcast.15, bf16[128,2048]{1,0:T(8,128)(2,1)} %bitcast.16, ...), custom_call_target="tpu_custom_call" | custom-call | tf_op jit(solution)/shard_map/pallas_call | solution.py:639
  92.0 1.4 %shard_map.111 = (bf16[128,2048]{1,0:T(8,128)(2,1)}, bf16[128,2048]{1,0:T(8,128)(2,1)}, bf16[128,2048]{1,0:T(8,128)(2,1)}, bf16[128,2048]{1,0:T(8,128)(2,1)}, f32[16,2048]{1,0:T(8,128)}) custom-call(bf16[128,2048]{1,0:T(8,128)(2,1)S(1)} %get-tuple-element.15.refs_0_, bf16[128,2048]{1,0:T(8,128)(2,1)S(1)} %get-tuple-element.16.refs_1_, ...), custom_call_target="tpu_custom_call" | custom-call | tf_op jit(solution)/shard_map/pallas_call | solution.py:650
Async XLA Ops:
  0.6 0.7 copy-start.2
  1.3 1.0 %copy-start = (bf16[1,128,2048]{2,1,0:T(8,128)(2,1)S(1)}, bf16[1,128,2048]{2,1,0:T(8,128)(2,1)}, u32[]{:S(2)}) copy-start(bf16[1,128,2048]{2,1,0:T(8,128)(2,1)} %param.7) | copy-start | bytes 1572868
  2.3 0.8 copy-start.1
